TPU v7x, 256 devices: a whole 4x4x8 slice. The times are simulated.
256 devices in a mesh: rep: 4 (over y_lo, core), dp: 64 (over x, y_hi, z).
Axes of the slice: x: 4, y: 4 (y_hi: 2, y_lo: 2; y = y_hi * 2 + y_lo), z: 8, core: 2. Of those that a mesh axis runs over, the one named last changes fastest.
Arguments:
- tokens: bfloat16 [32768, 80], P(('rep', 'dp')), may hold values from -6 to 6
- upstream: bfloat16 [32768, 80], P(('rep', 'dp')), may hold values from -6 to 6
- gate_pre: bfloat16 [32768, 14336], P(('rep', 'dp')), may hold values from -6 to 6
- up_pre: bfloat16 [32768, 14336], P(('rep', 'dp')), may hold values from -6 to 6
- param_shards: bfloat16 [34816, 128], P('dp'), may hold values from -0.625 to 0.625
- shard_rows: int32 [64], replicated, may hold values from 316 to 524, as said below
- row_state: float32 [240], replicated, may hold values from 1e-07 to 1e-05
- col_state: float32 [43008], replicated, may hold values from 1e-07 to 1e-05
Outputs:
- new_params: bfloat16 [34816, 128], P('dp')
- direction: bfloat16 [34816, 128], P('dp')
- new_rows: float32 [240], replicated
- new_cols: float32 [43008], replicated
Inputs may be any that keep to these rules, and one draw needn't show every extreme that they name: `shard_rows`: owner lengths of the flat buffer in order, summing to 26880; for every p below 64 - 1 the end of owner p lies within 52 rows of (p + 1) * 420; one owner holds exactly 524 rows.
All inputs are finite; a program needn't handle non-finite values.
Results may differ from a plain program's by a relative error of at most 0.0049.
Values may be sent and summed in bfloat16 or wider, within the bound.
A program may use at most 128 MiB of HBM per device.

v0:
```python
import jax
import jax.numpy as jnp
from jax import lax
from jax.sharding import PartitionSpec as P

BETA = 0.8
RHO = 0.2
TINY = 1e-30


def contract_rows(left, right):
    return lax.dot_general(
        left, right, (((0,), (0,)), ((), ())), preferred_element_type=jnp.float32
    )


def block_layout(shard_start, base, shard_len, count, bucket_rows, hidden_units):
    per_matrix = bucket_rows * hidden_units // 128
    offsets = base + jnp.arange(count, dtype=jnp.int32)
    live_rows = offsets < shard_len
    global_rows = jnp.minimum(shard_start + offsets, 3 * per_matrix - 1)
    matrix_id = (global_rows >= per_matrix).astype(jnp.int32) + (
        global_rows >= 2 * per_matrix
    ).astype(jnp.int32)
    inside = global_rows - matrix_id * per_matrix
    narrow = hidden_units // 128
    row_id = matrix_id * bucket_rows + inside // narrow
    col_block = matrix_id * narrow + inside % narrow
    return (live_rows, matrix_id, row_id, col_block)


def partial_factors(block, params_block, layout, bucket_rows, hidden_units):
    live_rows, matrix_id, row_id, col_block = layout
    squares = block * block
    row_part = jax.ops.segment_sum(
        jnp.where(live_rows, jnp.sum(squares, axis=1), 0.0), row_id, num_segments=3 * bucket_rows
    )
    col_part = jax.ops.segment_sum(
        jnp.where(live_rows[:, None], squares, 0.0), col_block, num_segments=3 * hidden_units // 128
    )
    weights = params_block.astype(jnp.float32)
    weight_rows = jnp.where(live_rows, jnp.sum(weights * weights, axis=1), 0.0)
    weight_sq = jnp.stack(
        [jnp.sum(jnp.where(matrix_id == number, weight_rows, 0.0)) for number in range(3)]
    )
    return (row_part, col_part, weight_sq)


def apply_update(
    block, params_block, layout, totals, row_state, col_state, bucket_rows, hidden_units
):
    live_rows, matrix_id, row_id, col_block = layout
    row_total, col_total, weight_sq = totals
    new_rows = BETA * row_state + (1.0 - BETA) * (row_total / float(hidden_units) + TINY)
    new_cols = BETA * col_state + (1.0 - BETA) * (col_total.reshape(-1) / float(bucket_rows) + TINY)
    row_means = jnp.mean(new_rows.reshape(3, bucket_rows), axis=1)
    scales = jnp.sqrt(weight_sq / float(bucket_rows * hidden_units))
    row_factor = jnp.take(new_rows, row_id) / jnp.take(row_means, matrix_id)
    col_factor = jnp.take(new_cols.reshape(-1, 128), col_block, axis=0)
    moved = block * lax.rsqrt(row_factor[:, None] * col_factor)
    updated = params_block.astype(jnp.float32) - RHO * jnp.take(scales, matrix_id)[:, None] * moved
    updated = jnp.where(live_rows[:, None], updated, 0.0).astype(jnp.bfloat16)
    moved = jnp.where(live_rows[:, None], moved, 0.0).astype(jnp.bfloat16)
    return (updated, moved, new_rows, new_cols)


def owner_layout(flat_grads, starts, shard_rows, capacity, rows_flat):
    owner_count = shard_rows.shape[0]
    offsets = jnp.arange(capacity, dtype=jnp.int32)
    indices = jnp.minimum(starts[:, None] + offsets[None, :], rows_flat - 1).reshape(-1)
    live_send = (offsets[None, :] < shard_rows[:, None]).reshape(-1)
    outgoing = jnp.where(live_send[:, None], jnp.take(flat_grads, indices, axis=0), 0.0)
    return outgoing.reshape(owner_count, capacity, 128)


def body(tokens, upstream, gate_pre, up_pre, param_shards, shard_rows, row_state, col_state):
    bucket_rows = tokens.shape[1]
    hidden_units = gate_pre.shape[1]
    data_size = lax.axis_size("dp")
    replica_size = lax.axis_size("rep")
    capacity = param_shards.shape[0]
    quarter = capacity // replica_size
    per_matrix = bucket_rows * hidden_units // 128
    rows_flat = 3 * per_matrix
    ends = jnp.cumsum(shard_rows)
    starts = ends - shard_rows
    owner_index = lax.axis_index("dp")
    replica_index = lax.axis_index("rep")
    shard_start = jnp.take(starts, owner_index)
    shard_len = jnp.take(shard_rows, owner_index)
    gathered = lax.all_gather(param_shards, "dp", axis=0, tiled=True)
    down_rows = 2 * per_matrix + jnp.arange(per_matrix, dtype=jnp.int32)
    owners = jnp.sum((ends[None, :] <= down_rows[:, None]).astype(jnp.int32), axis=1)
    positions = owners * capacity + down_rows - jnp.take(starts, owners)
    gate_in = gate_pre.astype(jnp.float32)
    up_in = up_pre.astype(jnp.float32)
    sigmoid_gate = jax.nn.sigmoid(gate_in)
    activated = gate_in * sigmoid_gate
    hidden = (activated * up_in).astype(jnp.bfloat16)
    grad_down = contract_rows(upstream, hidden)
    w_down = jnp.take(gathered, positions, axis=0).reshape(bucket_rows, hidden_units)
    d_hidden = jnp.dot(upstream, w_down, preferred_element_type=jnp.float32)
    d_gate = (d_hidden * up_in * sigmoid_gate * (1.0 + gate_in * (1.0 - sigmoid_gate))).astype(
        jnp.bfloat16
    )
    d_up = (d_hidden * activated).astype(jnp.bfloat16)
    grad_gate = contract_rows(tokens, d_gate)
    grad_up = contract_rows(tokens, d_up)
    flat_grads = jnp.concatenate(
        [grad_gate.reshape(-1, 128), grad_up.reshape(-1, 128), grad_down.reshape(-1, 128)], axis=0
    )
    outgoing = owner_layout(flat_grads, starts, shard_rows, capacity, rows_flat)
    owned = lax.psum_scatter(
        outgoing.reshape(data_size * capacity, 128), "dp", scatter_dimension=0, tiled=True
    )
    summed = lax.psum_scatter(owned, "rep", scatter_dimension=0, tiled=True)
    total_tokens = float(tokens.shape[0] * data_size * replica_size)
    summed = summed / total_tokens
    base = replica_index * quarter
    params_block = lax.dynamic_slice_in_dim(param_shards, base, quarter, 0)
    layout = block_layout(shard_start, base, shard_len, quarter, bucket_rows, hidden_units)
    parts = partial_factors(summed, params_block, layout, bucket_rows, hidden_units)
    totals = lax.psum((parts[0], parts[1], parts[2]), ("rep", "dp"))
    updated, moved, new_rows, new_cols = apply_update(
        summed, params_block, layout, totals, row_state, col_state, bucket_rows, hidden_units
    )
    new_params, direction = (
        lax.all_gather(updated, "rep", axis=0, tiled=True),
        lax.all_gather(moved, "rep", axis=0, tiled=True),
    )
    return (new_params, direction, new_rows, new_cols)


def solution(mesh):
    in_specs = (
        P(("rep", "dp"), None),
        P(("rep", "dp"), None),
        P(("rep", "dp"), None),
        P(("rep", "dp"), None),
        P("dp", None),
        P(),
        P(),
        P(),
    )
    out_specs = (P("dp", None), P("dp", None), P(), P())
    return jax.shard_map(body, mesh=mesh, in_specs=in_specs, out_specs=out_specs, check_vma=False)
```

profile of v0, /device:TPU:1, one launch (start us, length us, event | category | flops | bytes accessed | tf_op | source)
XLA Modules:
  0.0 1127.1 jit_solution(13369796267999596408)
XLA Ops:
  12.9 4.5 fusion.19
  18.8 6.4 compare_reduce_fusion.56
  25.2 36.2 %select_select_fusion.1 = s32[8960]{0:T(1024)S(1)} fusion(pred[8960]{0:T(1024)(128)(4,1)S(1)} %get-tuple-element.83, pred[8960]{0:T(1024)(128)(4,1)S(1)} %get-tuple-element.81, pred[8960]{0:T(1024)(128)(4,1)S(1)} %get-tuple-element.82, pred[8960]{0:T(1024)(128)(4,1)S(1)} %get-tuple-element.80, pred[8960]{0:T(1024)(128)(4,1)S(1)} %get-tuple-element.79, ...), kind=kLoop, calls=%fused_computation.119 | loop fusion | flops 510720 | bytes 582628 | tf_op jit(solution)/shard_map/jit(_take)/gather | solution.py:94
  61.5 6.2 copy.23
  67.7 6.1 copy.22
  73.8 7.8 convolution_bitcast_fusion.1
  81.6 5.5 reshape.323
  87.7 76.1 %all-gather.2.cloned.1.call-done = bf16[34816,128]{1,0:T(8,128)(2,1)} async-done(((bf16[544,128]{1,0:T(8,128)(2,1)}), bf16[34816,128]{1,0:T(8,128)(2,1)}) %all-gather.2.cloned.1.call-update) | async-done | bytes 8912912 | tf_op jit(solution)/shard_map/all_gather | solution.py:91
  163.8 22.0 %gather_fusion = bf16[8960,128]{1,0:T(8,128)(2,1)} fusion(bf16[34816,128]{1,0:T(8,128)(2,1)} %all-gather.2.cloned.1.call-done, s32[9216]{0:T(1024)S(1)} %pad_clamp_fusion), kind=kCustom, calls=%fused_computation | custom fusion | bytes 4623360 | tf_op jit(solution)/shard_map/jit(_take)/gather | solution.py:101
  185.7 2.9 gather.42
  192.5 3.9 convolution_bitcast_fusion.2
  196.4 5.0 convolution_bitcast_fusion.3
  201.4 5.4 reshape.321
  206.8 5.4 reshape.322
  212.2 12.3 %pad_maximum_fusion = f32[26880,128]{1,0:T(8,128)} fusion(f32[8960,128]{1,0:T(8,128)} %reshape.323, f32[8960,128]{1,0:T(8,128)} %reshape.322, f32[8960,128]{1,0:T(8,128)} %reshape.321), kind=kLoop, calls=%fused_computation.11 | loop fusion | flops 6881280 | bytes 27525120 | tf_op jit(solution)/shard_map/concatenate | solution.py:109
  224.5 120.5 %gather_fusion.1 = f32[34816,128]{1,0:T(8,128)} fusion(f32[26880,128]{1,0:T(8,128)} %pad_maximum_fusion, s32[34816]{0:T(1024)S(1)} %broadcast_clamp_fusion), kind=kCustom, calls=%fused_computation.1 | custom fusion | bytes 35790848 | tf_op jit(solution)/shard_map/jit(_take)/gather | solution.py:72
  345.1 14.3 %select_select_fusion = f32[34816,128]{1,0:T(8,128)} fusion(f32[34816,128]{1,0:T(8,128)} %gather_fusion.1, pred[34816]{0:T(1024)(128)(4,1)S(1)} %compare_and_fusion, pred[34816]{0:T(1024)(128)(4,1)S(1)} %lt.162), kind=kLoop, calls=%fused_computation.6 | loop fusion | flops 8912896 | bytes 35721216 | tf_op jit(solution)/shard_map/jit(_where)/select_n | solution.py:72
  362.1 351.2 %reduce-scatter.6.cloned.1.call-done = f32[544,128]{1,0:T(8,128)} async-done(((f32[34816,128]{1,0:T(8,128)}), f32[544,128]{1,0:T(8,128)}) %reduce-scatter.6.cloned.1.call-update) | async-done | bytes 278544 | tf_op jit(solution)/shard_map/reduce_scatter | solution.py:113
  713.5 64.2 %reduce-scatter.8.cloned.1.call-done = f32[136,128]{1,0:T(8,128)} async-done(((f32[544,128]{1,0:T(8,128)}), f32[136,128]{1,0:T(8,128)}) %reduce-scatter.8.cloned.1.call-update) | async-done | bytes 69648
  782.8 77.0 %all-reduce.1 = (f32[3]{0:T(128)S(1)}, f32[240]{0:T(256)S(1)}) all-reduce(f32[3]{0:T(128)S(1)} %pad_maximum_fusion.1, f32[240]{0:T(256)S(1)} %scatter_custom_fusion), channel_id=1, replica_groups=mesh['rep'=4,'dp'=64] {'rep','dp'}, use_global_device_ids=true, to_apply=%region_5.6 | all-reduce | flops 243 | bytes 1944 | tf_op jit(solution)/shard_map/psum | solution.py:123
  863.0 2.1 scatter_custom_fusion.1
  869.1 236.5 %all-reduce.4.cloned.1.call-done = f32[336,128]{1,0:T(8,128)} async-done(((f32[336,128]{1,0:T(8,128)}), f32[336,128]{1,0:T(8,128)}) %all-reduce.4.cloned.1.call-update) | async-done | bytes 172048 | tf_op jit(solution)/shard_map/psum | solution.py:123
  1108.3 5.5 all_gather.11
  1113.8 5.4 all_gather.10
  (83 shorter events, 29.1 us)
Async XLA Ops:
  7.2 66.6 %copy-start = (bf16[128,80]{0,1:T(8,128)(2,1)S(1)}, bf16[128,80]{0,1:T(8,128)(2,1)}, u32[]{:S(2)}) copy-start(bf16[128,80]{0,1:T(8,128)(2,1)} %param.11) | copy-start | bytes 61444
  7.2 156.6 %all-gather.2.cloned.1.call-start = ((), (), s32[]{:S(2)}) async-start(), calls=%async_computation.2 | async-start | bytes 9052160 | tf_op jit(solution)/shard_map/all_gather | solution.py:91
  7.9 705.4 %reduce-scatter.6.cloned.1.call-start = ((), (), s32[]{:S(2)}) async-start(), calls=%async_computation.3 | async-start | bytes 18104320 | tf_op jit(solution)/shard_map/reduce_scatter | solution.py:113
  190.4 2.0 copy-start.3
  190.4 2.0 copy-start.10
  192.5 4.0 copy-start.4
  359.3 761.2 %copy-start.1 = (bf16[128,80]{0,1:T(8,128)(2,1)S(1)}, bf16[128,80]{0,1:T(8,128)(2,1)}, u32[]{:S(2)}) copy-start(bf16[128,80]{0,1:T(8,128)(2,1)} %param.11) | copy-start | bytes 61444
  359.3 0.7 copy-start.8
  359.3 2.6 copy-start.6
  359.4 500.5 %copy-start.9 = (f32[240]{0:T(256)S(1)}, f32[240]{0:T(256)}, u32[]{:S(2)}) copy-start(f32[240]{0:T(256)} %param.16) | copy-start | bytes 2884
  359.4 746.2 %copy-start.7 = (f32[43008]{0:T(1024)S(1)}, f32[43008]{0:T(1024)}, u32[]{:S(2)}) copy-start(f32[43008]{0:T(1024)} %param.17) | copy-start | bytes 516100
  359.4 418.2 %reduce-scatter.8.cloned.1.call-start = ((), (), s32[]{:S(2)}) async-start(), calls=%async_computation.5 | async-start | bytes 348160
  713.3 392.3 %all-reduce.4.cloned.1.call-start = ((), (), s32[]{:S(2)}) async-start(), calls=%async_computation.4 | async-start | bytes 344064 | tf_op jit(solution)/shard_map/psum | solution.py:123
  859.9 260.7 %copy-start.2 = (f32[240]{0:T(256)}, f32[240]{0:T(256)S(1)}, u32[]{:S(2)}) copy-start(f32[240]{0:T(256)S(1)} %multiply_add_fusion) | copy-start | bytes 2884
  1106.6 14.0 %copy-start.5 = (f32[43008]{0:T(1024)}, f32[43008]{0:T(1024)S(1)}, u32[]{:S(2)}) copy-start(f32[43008]{0:T(1024)S(1)} %bitcast_add_fusion) | copy-start | bytes 516100
Sparse Core Ops, SparseCore 0:
  11.6 152.1 all-gather.1
  359.5 353.7 reduce-scatter.5
  716.0 61.6 reduce-scatter.7
  865.3 240.2 all-reduce.3
where the time goes:
time: 1130 us
  waiting for transfers between devices  729 us (65%)
  local copies, waits for them, and re-layouts  187 us (17%)
  other arithmetic  89.7 us (8%)
  blocking collectives  88 us (8%)
  matrix products  17.9 us (2%)
  between operations  15.4 us (1%)
    reduce_scatter x1, waiting for transfers between devices, body(): lax.psum_scatter(outgoing.reshape(data_size * capacity, 128), 'dp', scatt...  351 us
    psum x1, waiting for transfers between devices, body(): totals = lax.psum((parts[0], parts[1], parts[2]), ('rep', 'dp'))  237 us
    gather x1, local copies, waits for them, and re-layouts, owner_layout(): jnp.take(flat_grads, indices, axis=0)  121 us
    psum x1, blocking collectives, body(): totals = lax.psum((parts[0], parts[1], parts[2]), ('rep', 'dp'))  77 us
    all_gather x1, waiting for transfers between devices, body(): gathered = lax.all_gather(param_shards, 'dp', axis=0, tiled=True)  76.1 us
    unnamed x5, waiting for transfers between devices  64.9 us
    gather x3, other arithmetic, body(): positions = owners * capacity + down_rows - jnp.take(starts, owners)  47.1 us
    gather x2, local copies, waits for them, and re-layouts, body(): jnp.take(gathered, positions, axis=0).reshape(bucket_rows, hidden_units)  24.9 us
  transfers between devices with their start and end apart: 4, of which 4 were waited for; matrix products, arithmetic and copies ran while one was open for 7% of the time, Pallas kernels for 0%

commit v1 on v0

v1 whole, which is shorter than its diff:
```python
import functools

import jax
import jax.numpy as jnp
from jax import lax
from jax.experimental import pallas as pl
from jax.experimental.pallas import tpu as pltpu
from jax.sharding import PartitionSpec as P

BETA = 0.8
RHO = 0.2
TINY = 1e-30
RB = 80
NB = 112
EV = 420
JIT = 52
WIN = 528
FIRST = 42
NWIN = 22
PIECES = 7
SLOTS = 256
WPAD = 336
WROWS = 9360
F32 = jnp.float32
BF16 = jnp.bfloat16
VMEM_LIMIT = 56 * 1024 * 1024


def slot_row(pos):
    zz = pos % 4
    second = pos // 4 % 4
    first = pos // 16 % 4
    h = pos // 64 % 2
    core = pos // 128
    z = 2 * zz + h
    x, y = (first, second) if h == 0 else (second, first)
    p = (x * 2 + y // 2) * 8 + z
    r = (y % 2) * 2 + core
    q = (p % 4) * 4 + r
    return None if q == 15 else 15 * (p // 4) + q


def coords():
    r = lax.axis_index("rep")
    p = lax.axis_index("dp")
    x = p // 16
    y = (p // 8 % 2) * 2 + r // 2
    return x, y, p % 8, r % 2


def device(x, y, z, core):
    return {"rep": (y % 2) * 2 + core, "dp": (x * 2 + y // 2) * 8 + z}


def grads_kernel(tok_t, up_t, up, wwin, gate, upp, out, wflat, rows):
    c = pl.program_id(0)

    @pl.when(c == 0)
    def _():
        wflat[...] = jnp.zeros_like(wflat)
        for n in range(NWIN):
            off = EV * (FIRST + n) - JIT - 17920 + WPAD
            wflat[pl.ds(off, WIN), :] += wwin[n].astype(F32)

    def block(jj, carry):
        cols = pl.ds(pl.multiple_of(jj * 256, 256), 256)
        g = gate[:, cols].astype(F32)
        u = upp[:, cols].astype(F32)
        s = 0.5 * jnp.tanh(0.5 * g) + 0.5
        act = g * s
        hid = (act * u).astype(BF16)
        gd = jnp.dot(up_t[...], hid, preferred_element_type=F32)
        j = c * 16 + jj * 2
        w = jnp.concatenate(
            [wflat[pl.ds(WPAD + j + b, RB, stride=NB), :] for b in range(2)], axis=1
        ).astype(BF16)
        dh = jnp.dot(up[...], w, preferred_element_type=F32)
        dg = (dh * u * s * (1.0 + g * (1.0 - s))).astype(BF16)
        du = (dh * act).astype(BF16)
        gg = jnp.dot(tok_t[...], dg, preferred_element_type=F32)
        gu = jnp.dot(tok_t[...], du, preferred_element_type=F32)
        for m, v in enumerate((gg, gu, gd)):
            for b in range(2):
                rows[pl.ds(m * RB * 16 + jj * 2 + b, RB, stride=16), :] = v[:, b * 128 : b * 128 + 128]
        return carry

    lax.fori_loop(0, 8, block, 0)
    for pos in range(SLOTS):
        row = slot_row(pos)
        if row is None:
            out[0, pos] = jnp.zeros((16, 128), BF16)
        else:
            out[0, pos] = rows[row * 16 : row * 16 + 16, :].astype(BF16)


def grads(tokens, upstream, gate_pre, up_pre, wwin):
    whole = lambda shape: pl.BlockSpec(shape, lambda c: (0,) * len(shape))
    return pl.pallas_call(
        grads_kernel,
        grid=(PIECES,),
        in_specs=[
            whole((RB, 128)),
            whole((RB, 128)),
            whole((128, RB)),
            whole((NWIN, WIN, 128)),
            pl.BlockSpec((128, 2048), lambda c: (0, c)),
            pl.BlockSpec((128, 2048), lambda c: (0, c)),
        ],
        out_specs=pl.BlockSpec((1, SLOTS, 16, 128), lambda c: (c, 0, 0, 0)),
        out_shape=jax.ShapeDtypeStruct((PIECES, SLOTS, 16, 128), BF16),
        scratch_shapes=[pltpu.VMEM((WROWS, 128), F32), pltpu.VMEM((240 * 16, 128), F32)],
        compiler_params=pltpu.CompilerParams(vmem_limit_bytes=VMEM_LIMIT),
        name="grads",
    )(tokens.T, upstream.T, upstream, wwin, gate_pre, up_pre)


def greet(targets):
    barrier = pltpu.get_barrier_semaphore()
    for target in targets:
        pl.semaphore_signal(barrier, inc=1, device_id=target, device_id_type=pl.DeviceIdType.MESH)
    pl.semaphore_wait(barrier, len(targets))


def remote(src, dst, send, recv, target):
    return pltpu.make_async_remote_copy(
        src_ref=src, dst_ref=dst, send_sem=send, recv_sem=recv,
        device_id=target, device_id_type=pl.DeviceIdType.MESH,
    )


def scatter_kernel(f, out, c1, a1, c2, a2, a2own, c3, a3, c4, ss1, rs1, ss2, rs2, ss3, rs3, ss4, rs4):
    x, y, z, core = coords()
    axis_of = lambda h: (lambda d: device((x + d) % 4, y, z, core)) if h == 0 else (
        lambda d: device(x, (y + d) % 4, z, core))
    place = (x, y)
    greet(
        [device(x, y, z, 1 - core)]
        + [axis_of(h)(d) for h in range(2) for d in (1, 2, 3)]
        + [device(x, y, (z + d) % 8, core) for d in range(1, 8)]
    )

    def copy1(c):
        return remote(f.at[c, 1 - core], c1.at[c], ss1.at[c], rs1.at[c], device(x, y, z, 1 - core))

    def copy2(c, h, d):
        k = h * 3 + d - 1
        return remote(a1.at[c, h, (place[h] + d) % 4], c2.at[c, h, d - 1], ss2.at[c, k], rs2.at[c, k], axis_of(h)(d))

    def copy3(c, h, d):
        k = h * 3 + d - 1
        return remote(a2.at[c, h, (place[1 - h] + d) % 4], c3.at[c, h, d - 1], ss3.at[c, k], rs3.at[c, k], axis_of(1 - h)(d))

    def copy4(c, d):
        to = (z + d) % 8
        return remote(a3.at[c, to % 2, to // 2], c4.at[c, d - 1], ss4.at[c, d - 1], rs4.at[c, d - 1], device(x, y, to, core))

    def start1(c, carry):
        copy1(c).start()
        return carry

    def step1(c, carry):
        copy1(c).wait_recv()
        for h in range(2):
            def add(i, carry):
                a1[c, h, i] = (f[c, core, h, i].astype(F32) + c1[c, h, i].astype(F32)).astype(BF16)
                return carry
            lax.fori_loop(0, 4, add, 0)
            for d in (1, 2, 3):
                copy2(c, h, d).start()
        return carry

    def step2(c, carry):
        for h in range(2):
            for d in (1, 2, 3):
                copy2(c, h, d).wait_recv()
            def add(i, carry):
                v = f[c, core, h, place[h], pl.ds(i * 4, 4)].astype(F32) + c1[c, h, place[h], pl.ds(i * 4, 4)].astype(F32)
                for d in range(3):
                    v += c2[c, h, d, pl.ds(i * 4, 4)].astype(F32)
                a2[c, h, i] = v.astype(BF16)
                a2own[i] = v
                return carry
            lax.fori_loop(0, 4, add, 0)
            a3[c, h] = a2own[place[1 - h]]
            for d in (1, 2, 3):
                copy3(c, h, d).start()
        return carry

    def step3(c, carry):
        for h in range(2):
            for d in (1, 2, 3):
                copy3(c, h, d).wait_recv()
            v = a3[c, h]
            for d in range(3):
                v += c3[c, h, d].astype(F32)
            a3[c, h] = v
        for d in range(1, 8):
            copy4(c, d).start()
        return carry

    def step4(c, carry):
        for d in range(1, 8):
            copy4(c, d).wait_recv()
        v = a3[c, z % 2, z // 2]
        for d in range(7):
            v += c4[c, d]
        out[pl.ds(pl.multiple_of(c * 16, 16), 16), :] = v * (1.0 / 32768.0)
        return carry

    def drain(c, carry):
        copy1(c).wait_send()
        for h in range(2):
            for d in (1, 2, 3):
                copy2(c, h, d).wait_send()
                copy3(c, h, d).wait_send()
        for d in range(1, 8):
            copy4(c, d).wait_send()
        return carry

    for step in (start1, step1, step2, step3, step4, drain):
        lax.fori_loop(0, PIECES, step, 0)


def scatter(f):
    n = PIECES
    dma = pltpu.SemaphoreType.DMA
    return pl.pallas_call(
        scatter_kernel,
        in_specs=[pl.BlockSpec(memory_space=pltpu.VMEM)],
        out_specs=pl.BlockSpec(memory_space=pltpu.VMEM),
        out_shape=jax.ShapeDtypeStruct((NB, 128), F32),
        scratch_shapes=[
            pltpu.VMEM((n, 2, 4, 16, 16, 128), BF16),
            pltpu.VMEM((n, 2, 4, 16, 16, 128), BF16),
            pltpu.VMEM((n, 2, 3, 16, 16, 128), BF16),
            pltpu.VMEM((n, 2, 4, 4, 16, 128), BF16),
            pltpu.VMEM((4, 4, 16, 128), F32),
            pltpu.VMEM((n, 2, 3, 4, 16, 128), BF16),
            pltpu.VMEM((n, 2, 4, 16, 128), F32),
            pltpu.VMEM((n, 7, 16, 128), F32),
            dma((n,)), dma((n,)), dma((n, 6)), dma((n, 6)), dma((n, 6)), dma((n, 6)), dma((n, 7)), dma((n, 7)),
        ],
        compiler_params=pltpu.CompilerParams(
            vmem_limit_bytes=VMEM_LIMIT, collective_id=0, has_side_effects=True
        ),
        name="scatter",
    )(f.reshape(n, 2, 2, 4, 16, 16, 128))


BASES = (-1, 3, 7, 10)
COUNTS = (6, 5, 5, 6)


def sums_kernel(g, wext, gw, cols, extra, s, pa, acc, pb, tot, pc, ssa, rsa, ssb, rsb, ssc, rsc, ssg, rsg):
    x, y, z, core = coords()
    r = lax.axis_index("rep")
    p = lax.axis_index("dp")
    group, a = p // 4, p % 4
    q = a * 4 + r
    row = 15 * group + q
    ka, kb = z * 2 + core, x * 4 + y
    in_a = lambda d: (lambda k: device(x, y, k // 2, k % 2))((ka + d) % 16)
    in_b = lambda d: (lambda k: device(k // 4, k % 4, z, core))((kb + d) % 16)

    barrier = pltpu.get_barrier_semaphore()

    def hello(target):
        pl.semaphore_signal(barrier, inc=1, device_id=target, device_id_type=pl.DeviceIdType.MESH)

    for d in range(1, 16):
        hello(in_a(d))
        hello(in_b(d))
    hello({"rep": 3 - r, "dp": p})

    @pl.when(p > 0)
    def _():
        for k in range(4):
            hello({"rep": k, "dp": jnp.maximum(p - 1, 0)})

    @pl.when(p < 63)
    def _():
        for k in range(4):
            hello({"rep": k, "dp": jnp.minimum(p + 1, 63)})

    pl.semaphore_wait(barrier, 31 + 4 * jnp.where(p > 0, 1, 0) + 4 * jnp.where(p < 63, 1, 0))

    def give(fn):
        for t in range(6):
            if t < 4:
                owner, k = 4 * group + t, q - BASES[t]
                ok = (k >= 0) & (k < COUNTS[t]) & (q < 15)
                k = jnp.clip(k, 0, 5)
            elif t == 4:
                owner, k, ok = jnp.maximum(p - a - 1, 0), 5, (q == 0) & (p > 0)
            else:
                owner, k, ok = jnp.minimum(p - a + 4, 63), 0, (q == 14) & (p < 60)
            for rr in range(4):
                fn(owner, k, ok, rr, t * 4 + rr)

    def send_row(owner, k, ok, rr, n):
        @pl.when(ok & ((owner != p) | (rr != r)))
        def _():
            remote(g, gw.at[k], ssg.at[n], rsg.at[k], {"rep": rr, "dp": owner}).start()
        @pl.when(ok & (owner == p) & (rr == r))
        def _():
            gw[k] = g[...]

    give(send_row)

    sq = g[...] * g[...]
    total = jnp.sum(sq)
    lane = lax.broadcasted_iota(jnp.int32, (1, 128), 1)
    last = jnp.where(lane == row % RB, total, 0.0) * jnp.where(q < 15, 1.0, 0.0) + wext[0:1, :]
    for k in range(16):
        s[k, 0:7, :] = sq[7 * k : 7 * k + 7, :]
        s[k, 7:8, :] = last

    def copy_a(d):
        return remote(s.at[(ka + d) % 16], pa.at[d - 1], ssa.at[d - 1], rsa.at[d - 1], in_a(d))

    def copy_b(d):
        return remote(acc, pb.at[d - 1], ssb.at[d - 1], rsb.at[d - 1], in_b(d))

    def copy_c(d):
        return remote(tot, pc.at[d - 1], ssc.at[d - 1], rsc.at[d - 1], in_a(d))

    for d in range(1, 16):
        copy_a(d).start()

    def matrix_at(k):
        pp = p - z + k // 2
        rr = r - core + k % 2
        return jnp.minimum(15 * (pp // 4) + (pp % 4) * 4 + rr, 239) // RB

    v = s[ka]
    own = matrix_at(ka)
    for m in range(3):
        acc[m] = jnp.where(own == m, v, 0.0)
    for d in range(1, 16):
        copy_a(d).wait_recv()
        v = pa[d - 1]
        m_src = matrix_at((ka + 16 - d) % 16)
        for m in range(3):
            acc[m] += jnp.where(m_src == m, v, 0.0)
    for d in range(1, 16):
        copy_b(d).start()
    tot[...] = acc[...]
    for d in range(1, 16):
        copy_b(d).wait_recv()
        tot[...] += pb[d - 1]
    for d in range(1, 16):
        copy_c(d).start()

    def place(k, v):
        for m in range(3):
            cols[m, k] = v[m]

    place(ka, tot[...])
    extra[...] = tot[...]
    for d in range(1, 16):
        copy_c(d).wait_recv()
        place((ka + 16 - d) % 16, pc[d - 1])

    for k in range(6):
        if k == 0:
            ok = (p % 4 != 0) | (p > 0)
        elif k == 5:
            ok = (a == 0) | ((a == 3) & (p < 63))
        else:
            ok = a >= 0
        source_q = jnp.where(a == 0, k - 1, jnp.where(a == 1, k + 3, jnp.where(a == 2, k + 7, k + 10)))
        @pl.when(ok & ((source_q != q) | (source_q > 14)))
        def _():
            remote(g, gw.at[k], ssg.at[k], rsg.at[k], {"rep": (r + 1) % 4, "dp": p}).wait_recv()
        @pl.when(jnp.logical_not(ok))
        def _():
            gw[k] = jnp.zeros((NB, 128), F32)

    def wait_row(owner, k, ok, rr, n):
        @pl.when(ok & ((owner != p) | (rr != r)))
        def _():
            remote(g, gw.at[k], ssg.at[n], rsg.at[k], {"rep": rr, "dp": owner}).wait_send()

    give(wait_row)
    for d in range(1, 16):
        copy_a(d).wait_send()
        copy_b(d).wait_send()
        copy_c(d).wait_send()


def sums(g, wext):
    dma = pltpu.SemaphoreType.DMA
    vm = pl.BlockSpec(memory_space=pltpu.VMEM)
    return pl.pallas_call(
        sums_kernel,
        in_specs=[vm, vm],
        out_specs=[vm, vm, vm],
        out_shape=[
            jax.ShapeDtypeStruct((6, NB, 128), F32),
            jax.ShapeDtypeStruct((3, 16, 8, 128), F32),
            jax.ShapeDtypeStruct((3, 8, 128), F32),
        ],
        scratch_shapes=[
            pltpu.VMEM((16, 8, 128), F32),
            pltpu.VMEM((15, 8, 128), F32),
            pltpu.VMEM((3, 8, 128), F32),
            pltpu.VMEM((15, 3, 8, 128), F32),
            pltpu.VMEM((3, 8, 128), F32),
            pltpu.VMEM((15, 3, 8, 128), F32),
            dma((15,)), dma((15,)), dma((15,)), dma((15,)), dma((15,)), dma((15,)), dma((24,)), dma((6,)),
        ],
        compiler_params=pltpu.CompilerParams(
            vmem_limit_bytes=VMEM_LIMIT, collective_id=1, has_side_effects=True
        ),
        name="sums",
    )(g, wext)


def update_kernel(place, gw, cols, extra, params, row_state, col_state, out_p, out_d, out_r, out_c, moved, scaled):
    shift, length, first = place[0], place[1], place[2]
    for m in range(3):
        for k in range(16):
            part = pl.ds(m * NB + 7 * k, 7)
            out_c[part, :] = BETA * col_state[part, :] + (1.0 - BETA) * (cols[m, k, 0:7, :] * (1.0 / RB) + TINY)
    lane = lax.broadcasted_iota(jnp.int32, (1, 128), 1)
    sums_row = extra[:, 7, :]
    live = lax.broadcasted_iota(jnp.int32, (3, 128), 1) < RB
    rows = jnp.where(live, BETA * row_state[...] + (1.0 - BETA) * (sums_row * (1.0 / 14336.0) + TINY), 0.0)
    out_r[...] = rows
    means = jnp.sum(rows, axis=1, keepdims=True) * (1.0 / RB)
    weight = jnp.sum(sums_row, axis=0, keepdims=True)
    for k in range(6):
        row = jnp.clip(first + k, 0, 239)
        m = row // RB
        i = row % RB
        pick = lambda v: jnp.where(m == 0, v[0:1], jnp.where(m == 1, v[1:2], v[2:3]))
        value = jnp.sum(jnp.where(lane == i, pick(rows), 0.0), axis=1, keepdims=True)
        sq = jnp.sum(jnp.where(lane == 120 + m, weight, 0.0), axis=1, keepdims=True)
        scale = RHO * jnp.sqrt(sq * (1.0 / (RB * 14336.0)))
        factor = value / pick(means)
        v = gw[k] * lax.rsqrt(factor * out_c[pl.ds(pl.multiple_of(m * NB, 8), NB), :])
        moved[pl.ds(k * NB, NB), :] = v
        scaled[pl.ds(k * NB, NB), :] = scale * v
    def tile(t, carry):
        o = pl.multiple_of(t * 16, 16)
        at = pl.ds(shift + o, 16)
        keep = o + lax.broadcasted_iota(jnp.int32, (16, 128), 0) < length
        out_d[pl.ds(o, 16), :] = jnp.where(keep, moved[at, :], 0.0).astype(BF16)
        new = params[pl.ds(o, 16), :].astype(F32) - scaled[at, :]
        out_p[pl.ds(o, 16), :] = jnp.where(keep, new, 0.0).astype(BF16)
        return carry
    lax.fori_loop(0, 34, tile, 0)


def update(place, gw, cols, extra, params, row_state, col_state):
    vm = pl.BlockSpec(memory_space=pltpu.VMEM)
    return pl.pallas_call(
        update_kernel,
        in_specs=[pl.BlockSpec(memory_space=pltpu.SMEM)] + [vm] * 6,
        out_specs=[vm] * 4,
        out_shape=[
            jax.ShapeDtypeStruct((544, 128), BF16),
            jax.ShapeDtypeStruct((544, 128), BF16),
            jax.ShapeDtypeStruct((3, 128), F32),
            jax.ShapeDtypeStruct((336, 128), F32),
        ],
        scratch_shapes=[pltpu.VMEM((800, 128), F32), pltpu.VMEM((800, 128), F32)],
        compiler_params=pltpu.CompilerParams(vmem_limit_bytes=VMEM_LIMIT),
        name="update",
    )(place, gw, cols, extra, params, row_state, col_state)


def body(tokens, upstream, gate_pre, up_pre, param_shards, shard_rows, row_state, col_state):
    p = lax.axis_index("dp")
    ends = jnp.cumsum(shard_rows)
    start = ends[p] - shard_rows[p]
    length = shard_rows[p]
    capacity = param_shards.shape[0]
    offsets = jnp.arange(capacity, dtype=jnp.int32)[:, None]
    masked = jnp.where(offsets < length, param_shards, jnp.zeros_like(param_shards))
    window = lax.dynamic_slice_in_dim(
        jnp.pad(masked, ((2 * JIT, 0), (0, 0))), 2 * JIT - (start - (EV * p - JIT)), WIN, 0
    )
    wwin = lax.all_gather(window, "dp", axis=0)[FIRST:]
    squares = jnp.sum(jnp.square(masked.astype(F32)), axis=1, keepdims=True)
    flat = start + offsets
    parts = [jnp.sum(jnp.where((flat >= m * 8960) & (flat < m * 8960 + 8960), squares, 0.0)) for m in range(3)]
    lane = jnp.arange(128)[None, :]
    wext = sum(jnp.where(lane == 120 + m, parts[m] * 0.25, 0.0) for m in range(3))
    wext = jnp.broadcast_to(wext, (8, 128))
    f = grads(tokens, upstream, gate_pre, up_pre, wwin)
    g = scatter(f)
    gw, cols, extra = sums(g, wext)
    a = p % 4
    first = 15 * (p // 4) + jnp.where(a == 0, -1, jnp.where(a == 1, 3, jnp.where(a == 2, 7, 10)))
    place = jnp.stack([start - NB * first, length, first]).astype(jnp.int32)
    row_in = jnp.pad(row_state.reshape(3, RB), ((0, 0), (0, 128 - RB)))
    new_params, direction, rows, new_cols = update(
        place, gw, cols, extra, param_shards, row_in, col_state.reshape(336, 128)
    )
    return (new_params, direction, rows[:, :RB].reshape(-1), new_cols.reshape(-1))


def solution(mesh):
    in_specs = (
        P(("rep", "dp"), None),
        P(("rep", "dp"), None),
        P(("rep", "dp"), None),
        P(("rep", "dp"), None),
        P("dp", None),
        P(),
        P(),
        P(),
    )
    out_specs = (P("dp", None), P("dp", None), P(), P())
    return jax.shard_map(body, mesh=mesh, in_specs=in_specs, out_specs=out_specs, check_vma=False)
```

time: 1130 us -> 281 us (0.25)
  waiting for transfers between devices: 729 us -> 144 us
  local copies, waits for them, and re-layouts: 187 us -> 11 us
  Pallas kernels: 0 us -> 105 us
  blocking collectives: 88 us -> 0 us
  other arithmetic: 89.7 us -> 3.79 us
  matrix products: 17.9 us -> 0 us
    reduce_scatter x1 -> x0, waiting for transfers between devices: 351 us -> none  [body(): lax.psum_scatter(outgoing.reshape(data_size * capacity, 128), 'dp', scatt...]
    psum x1 -> x0, waiting for transfers between devices: 237 us -> none  [body(): totals = lax.psum((parts[0], parts[1], parts[2]), ('rep', 'dp'))]
    gather x12 -> x0, local copies, waits for them, and re-layouts: 152 us -> none  [the longest x1 121 us: owner_layout(): jnp.take(flat_grads, indices, axis=0)]
    pallas_call x0 -> x4, Pallas kernels: none -> 105 us  [the longest x1 49.8 us: scatter(): pl.pallas_call(scatter_kernel, in_specs=[pl.BlockSpec(memory_space=pltpu....]
    psum x1 -> x0, blocking collectives: 77 us -> none  [body(): totals = lax.psum((parts[0], parts[1], parts[2]), ('rep', 'dp'))]
    all_gather x1, waiting for transfers between devices: 76.1 us -> 144 us  [body(): wwin = lax.all_gather(window, 'dp', axis=0)[FIRST:]]
    unnamed x5 -> x1, waiting for transfers between devices: 64.9 us -> 0.02 us
    gather x7 -> x0, other arithmetic: 47.1 us -> none  [the longest x3 47.1 us: body(): positions = owners * capacity + down_rows - jnp.take(starts, owners)]
  transfers between devices with their start and end apart: 4 -> 1, of which waited for: 4 -> 1; matrix products, arithmetic and copies ran while one was open for 7% -> 2% of each run, Pallas kernels for 0% -> 0%
where the time goes in v1:
time: 281 us
  waiting for transfers between devices  144 us (51%)
  Pallas kernels  105 us (37%)
  between operations  17.3 us (6%)
  local copies, waits for them, and re-layouts  11 us (4%)
  other arithmetic  3.79 us (1%)
    all_gather x1, waiting for transfers between devices, body(): wwin = lax.all_gather(window, 'dp', axis=0)[FIRST:]  144 us
    pallas_call x1, Pallas kernels, scatter(): pl.pallas_call(scatter_kernel, in_specs=[pl.BlockSpec(memory_space=pltpu....  49.8 us
    pallas_call x1, Pallas kernels, sums(): pl.pallas_call(sums_kernel, in_specs=[vm, vm], out_specs=[vm, vm, vm], ou...  27.7 us
    pallas_call x1, Pallas kernels, grads(): pl.pallas_call(grads_kernel, grid=(PIECES,), in_specs=[whole((RB, 128)),...  24.5 us
  transfers between devices with their start and end apart: 1, of which 1 were waited for; matrix products, arithmetic and copies ran while one was open for 2% of the time, Pallas kernels for 0%

profile of v1, /device:TPU:1, one launch (start us, length us, event | category | flops | bytes accessed | tf_op | source)
XLA Modules:
  0.0 280.6 jit_solution(6692801891711853707)
XLA Ops:
  7.2 0.0 all-gather.3.cloned.1.call-start
  7.2 1.2 dynamic_slice.11
  8.5 0.7 copy.12
  9.2 0.1 reduce-window.4
  9.3 0.5 constant_dynamic-slice_fusion
  9.8 0.6 iota_compare_fusion
  11.8 1.2 multiply_reduce_fusion
  12.9 0.7 pad_dynamic-slice_fusion
  13.7 0.0 all-gather.3.cloned.1.call-update
  13.7 1.4 copy.13.up
  15.2 0.6 select_reduce_fusion.2
  17.7 0.8 reshape.79
  18.4 0.5 pad.9.row_state
  19.0 1.3 pad_add_fusion.place
  20.2 143.9 %all-gather.3.cloned.1.call-done = bf16[33792,128]{1,0:T(8,128)(2,1)} async-done(((bf16[528,128]{1,0:T(8,128)(2,1)}), bf16[33792,128]{1,0:T(8,128)(2,1)}) %all-gather.3.cloned.1.call-update) | async-done | bytes 8650768 | tf_op jit(solution)/shard_map/all_gather | solution.py:484
  164.1 3.2 %slice.9 = bf16[11616,128]{1,0:T(8,128)(2,1)} slice(bf16[33792,128]{1,0:T(8,128)(2,1)} %all-gather.3.cloned.1.call-done), slice={[22176:33792], [0:128]} | slice | bytes 5947392 | tf_op jit(solution)/shard_map/slice | solution.py:484
  167.3 24.5 %grads.1 = bf16[7,256,16,128]{3,2,1,0:T(8,128)(2,1)} custom-call(bf16[80,128]{1,0:T(8,128)(2,1)} %bitcast.16, bf16[80,128]{1,0:T(8,128)(2,1)} %bitcast.15, bf16[128,80]{1,0:T(8,128)(2,1)} %copy.13.up, bf16[22,528,128]{2,1,0:T(8,128)(2,1)} %bitcast.13, bf16[128,14336]{1,0:T(8,128)(2,1)} %gate.1, bf16[128,14336]{1,0:T(8,128)(2,1)} %upp.1), custom_call_target="tpu_custom_call" | custom-call | tf_op jit(solution)/shard_map/grads/pallas_call | solution.py:98
  191.8 49.8 %scatter.1.g = f32[112,128]{1,0:T(8,128)} custom-call(bf16[7,2,2,4,16,16,128]{6,5,4,3,2,1,0:T(8,128)(2,1)} %bitcast.12), custom_call_target="tpu_custom_call" | custom-call | tf_op jit(solution)/shard_map/scatter/pallas_call | solution.py:227
  241.6 0.6 broadcast_in_dim.48.wext
  242.2 27.7 %sums.1 = (f32[6,112,128]{2,1,0:T(8,128)}, f32[3,16,8,128]{3,2,1,0:T(8,128)}, f32[3,8,128]{2,1,0:T(8,128)}) custom-call(f32[112,128]{1,0:T(8,128)} %scatter.1.g, f32[8,128]{1,0:T(8,128)} %broadcast_in_dim.48.wext), custom_call_target="tpu_custom_call" | custom-call | tf_op jit(solution)/shard_map/sums/pallas_call | solution.py:394
  270.0 2.5 update.1
  272.5 1.3 reshape.81
  (1 shorter events, 0.0 us)
Async XLA Ops:
  7.2 156.9 %all-gather.3.cloned.1.call-start = ((), (), s32[]{:S(2)}) async-start(), calls=%async_computation | async-start | bytes 8785920 | tf_op jit(solution)/shard_map/all_gather | solution.py:484
Sparse Core Ops, SparseCore 0:
  13.8 150.2 all-gather.2

commit v2 on v1

--- a/solution.py
+++ b/solution.py
@@ -52,15 +52,161 @@
     return {"rep": (y % 2) * 2 + core, "dp": (x * 2 + y // 2) * 8 + z}
 
 
+def span(lengths):
+    p = lax.axis_index("dp")
+    start = lax.fori_loop(0, p, lambda k, total: total + lengths[k], jnp.int32(0))
+    return start, lengths[p]
+
+
+def prep_kernel(lengths, params, quarter, wext, shifted):
+    p, r = lax.axis_index("dp"), lax.axis_index("rep")
+    start, length = span(lengths)
+    row = lax.broadcasted_iota(jnp.int32, (544, 128), 0)
+    v = jnp.where(row < length, params[...].astype(F32), 0.0)
+    shifted[0 : 2 * JIT, :] = jnp.zeros((2 * JIT, 128), F32)
+    shifted[2 * JIT : 2 * JIT + 544, :] = v
+    shifted[2 * JIT + 544 :, :] = jnp.zeros((72, 128), F32)
+    at = 2 * JIT - (start - (EV * p - JIT)) + 144 * r
+    quarter[...] = shifted[pl.ds(at, 144), :].astype(BF16)
+    v = v * v
+    flat = row + start
+    lane = lax.broadcasted_iota(jnp.int32, (8, 128), 1)
+    total = jnp.zeros((8, 128), F32)
+    for m in range(3):
+        inside = (flat >= m * 8960) & (flat < m * 8960 + 8960)
+        total += jnp.where(lane == 120 + m, 0.25 * jnp.sum(jnp.where(inside, v, 0.0)), 0.0)
+    wext[...] = total
+
+
+def prep(shard_rows, params):
+    vm = pl.BlockSpec(memory_space=pltpu.VMEM)
+    return pl.pallas_call(
+        prep_kernel,
+        in_specs=[pl.BlockSpec(memory_space=pltpu.SMEM), vm],
+        out_specs=[vm, vm],
+        out_shape=[jax.ShapeDtypeStruct((144, 128), BF16), jax.ShapeDtypeStruct((8, 128), F32)],
+        scratch_shapes=[pltpu.VMEM((720, 128), F32)],
+        compiler_params=pltpu.CompilerParams(vmem_limit_bytes=VMEM_LIMIT),
+        name="prep",
+    )(shard_rows, params)
+
+
+def gather_kernel(quarter, w, s1, r1, sp, rp, sm, rm, sy, ry, sc, rc):
+    x, y, z, core = coords()
+    r, p = lax.axis_index("rep"), lax.axis_index("dp")
+    plane = p // 8
+    spread = lambda d: {"rep": r, "dp": (plane + d) % 8 * 8 + z}
+    up, down = device(x, y, (z + 1) % 8, core), device(x, y, (z + 7) % 8, core)
+    north, south = device(x, (y + 1) % 4, z, core), device(x, (y + 3) % 4, z, core)
+    other = device(x, y, z, 1 - core)
+    greet([spread(d) for d in range(1, 8)] + [up, down, north, south, other])
+    mate = (1 - r // 2) * 2 + core
+
+    def copy1(d):
+        u = jnp.maximum(plane - 5, 0)
+        return remote(quarter, w.at[z, r, u], s1.at[d - 1], r1.at[u], spread(d))
+
+    def copy_up(s):
+        o = (z + 9 - s) % 8
+        return remote(w.at[o, r], w.at[o, r], sp.at[s - 1], rp.at[s - 1], up)
+
+    def copy_down(s):
+        o = (z + s - 1) % 8
+        return remote(w.at[o, r], w.at[o, r], sm.at[s - 1], rm.at[s - 1], down)
+
+    def copy_y(k):
+        o = (z + 8 - k) % 8
+        to = south if k in (0, 5, 6, 7) else north
+        return remote(w.at[o, r], w.at[o, r], sy.at[k], ry.at[k], to)
+
+    def copy_core(k, quarter_of, n):
+        o = (z + 8 - k) % 8
+        return remote(w.at[o, quarter_of], w.at[o, quarter_of], sc.at[n], rc.at[n], other)
+
+    holds = p >= 40
+
+    @pl.when(holds)
+    def _():
+        for d in range(1, 8):
+            copy1(d).start()
+        w[z, r, jnp.maximum(plane - 5, 0)] = quarter[...]
+
+    for u in range(3):
+        @pl.when(plane != 5 + u)
+        def _():
+            remote(quarter, w.at[z, r, u], s1.at[0], r1.at[u], spread(1)).wait_recv()
+
+    copy_up(1).start()
+    copy_down(1).start()
+    copy_y(0).start()
+    copy_core(0, r, 0).start()
+    for s in range(1, 5):
+        copy_up(s).wait_recv()
+        if s < 4:
+            copy_up(s + 1).start()
+        copy_y(s).start()
+        copy_core(s, r, s).start()
+        if s < 4:
+            copy_down(s).wait_recv()
+            if s < 3:
+                copy_down(s + 1).start()
+            copy_y(8 - s).start()
+            copy_core(8 - s, r, 8 - s).start()
+    for k in (0, 1, 7, 2, 6, 3, 5, 4):
+        copy_y(k).wait_recv()
+        copy_core(k, mate, 8 + k).start()
+    for k in range(8):
+        copy_core(k, r, k).wait_recv()
+        copy_core(k, mate, 8 + k).wait_recv()
+
+    @pl.when(holds)
+    def _():
+        for d in range(1, 8):
+            copy1(d).wait_send()
+
+    for s in range(1, 5):
+        copy_up(s).wait_send()
+        if s < 4:
+            copy_down(s).wait_send()
+    for k in range(8):
+        copy_y(k).wait_send()
+        copy_core(k, r, k).wait_send()
+        copy_core(k, mate, 8 + k).wait_send()
+
+
+def gather(quarter):
+    dma = pltpu.SemaphoreType.DMA
+    vm = pl.BlockSpec(memory_space=pltpu.VMEM)
+    return pl.pallas_call(
+        gather_kernel,
+        in_specs=[vm],
+        out_specs=vm,
+        out_shape=jax.ShapeDtypeStruct((8, 4, 3, 144, 128), BF16),
+        scratch_shapes=[dma((n,)) for n in (7, 3, 4, 4, 3, 3, 8, 8, 16, 16)],
+        compiler_params=pltpu.CompilerParams(
+            vmem_limit_bytes=VMEM_LIMIT, collective_id=2, has_side_effects=True
+        ),
+        name="gather",
+    )(quarter)
+
+
 def grads_kernel(tok_t, up_t, up, wwin, gate, upp, out, wflat, rows):
     c = pl.program_id(0)
 
     @pl.when(c == 0)
     def _():
-        wflat[...] = jnp.zeros_like(wflat)
         for n in range(NWIN):
             off = EV * (FIRST + n) - JIT - 17920 + WPAD
-            wflat[pl.ds(off, WIN), :] += wwin[n].astype(F32)
+            u, zz = (FIRST + n - 40) // 8, (FIRST + n) % 8
+            for r in range(4):
+                for t in range(9 if r < 3 else 6):
+                    v = wwin[zz, r, u, t * 16 : t * 16 + 16, :].astype(F32)
+                    first = r * 144 + t * 16
+                    for half in range(2):
+                        if n and first + half * 8 < 2 * JIT:
+                            wflat[pl.ds(off + first + half * 8, 8), :] += v[half * 8 : half * 8 + 8]
+                        else:
+                            wflat[pl.ds(off + first + half * 8, 8), :] = v[half * 8 : half * 8 + 8]
 
     def block(jj, carry):
         cols = pl.ds(pl.multiple_of(jj * 256, 256), 256)
@@ -102,7 +248,7 @@
             whole((RB, 128)),
             whole((RB, 128)),
             whole((128, RB)),
-            whole((NWIN, WIN, 128)),
+            whole((8, 4, 3, 144, 128)),
             pl.BlockSpec((128, 2048), lambda c: (0, c)),
             pl.BlockSpec((128, 2048), lambda c: (0, c)),
         ],
@@ -416,8 +562,12 @@
     )(g, wext)
 
 
-def update_kernel(place, gw, cols, extra, params, row_state, col_state, out_p, out_d, out_r, out_c, moved, scaled):
-    shift, length, first = place[0], place[1], place[2]
+def update_kernel(lengths, gw, cols, extra, params, row_state, col_state, out_p, out_d, out_r, out_c, moved, scaled):
+    p = lax.axis_index("dp")
+    start, length = span(lengths)
+    a = p % 4
+    first = 15 * (p // 4) + jnp.where(a == 0, -1, jnp.where(a == 1, 3, jnp.where(a == 2, 7, 10)))
+    shift = start - NB * first
     for m in range(3):
         for k in range(16):
             part = pl.ds(m * NB + 7 * k, 7)
@@ -452,7 +602,7 @@
     lax.fori_loop(0, 34, tile, 0)
 
 
-def update(place, gw, cols, extra, params, row_state, col_state):
+def update(lengths, gw, cols, extra, params, row_state, col_state):
     vm = pl.BlockSpec(memory_space=pltpu.VMEM)
     return pl.pallas_call(
         update_kernel,
@@ -467,36 +617,18 @@
         scratch_shapes=[pltpu.VMEM((800, 128), F32), pltpu.VMEM((800, 128), F32)],
         compiler_params=pltpu.CompilerParams(vmem_limit_bytes=VMEM_LIMIT),
         name="update",
-    )(place, gw, cols, extra, params, row_state, col_state)
+    )(lengths, gw, cols, extra, params, row_state, col_state)
 
 
 def body(tokens, upstream, gate_pre, up_pre, param_shards, shard_rows, row_state, col_state):
-    p = lax.axis_index("dp")
-    ends = jnp.cumsum(shard_rows)
-    start = ends[p] - shard_rows[p]
-    length = shard_rows[p]
-    capacity = param_shards.shape[0]
-    offsets = jnp.arange(capacity, dtype=jnp.int32)[:, None]
-    masked = jnp.where(offsets < length, param_shards, jnp.zeros_like(param_shards))
-    window = lax.dynamic_slice_in_dim(
-        jnp.pad(masked, ((2 * JIT, 0), (0, 0))), 2 * JIT - (start - (EV * p - JIT)), WIN, 0
-    )
-    wwin = lax.all_gather(window, "dp", axis=0)[FIRST:]
-    squares = jnp.sum(jnp.square(masked.astype(F32)), axis=1, keepdims=True)
-    flat = start + offsets
-    parts = [jnp.sum(jnp.where((flat >= m * 8960) & (flat < m * 8960 + 8960), squares, 0.0)) for m in range(3)]
-    lane = jnp.arange(128)[None, :]
-    wext = sum(jnp.where(lane == 120 + m, parts[m] * 0.25, 0.0) for m in range(3))
-    wext = jnp.broadcast_to(wext, (8, 128))
+    quarter, wext = prep(shard_rows, param_shards)
+    wwin = gather(quarter)
     f = grads(tokens, upstream, gate_pre, up_pre, wwin)
     g = scatter(f)
     gw, cols, extra = sums(g, wext)
-    a = p % 4
-    first = 15 * (p // 4) + jnp.where(a == 0, -1, jnp.where(a == 1, 3, jnp.where(a == 2, 7, 10)))
-    place = jnp.stack([start - NB * first, length, first]).astype(jnp.int32)
     row_in = jnp.pad(row_state.reshape(3, RB), ((0, 0), (0, 128 - RB)))
     new_params, direction, rows, new_cols = update(
-        place, gw, cols, extra, param_shards, row_in, col_state.reshape(336, 128)
+        shard_rows, gw, cols, extra, param_shards, row_in, col_state.reshape(336, 128)
     )
     return (new_params, direction, rows[:, :RB].reshape(-1), new_cols.reshape(-1))
 

time: 281 us -> 149 us (0.53)
  waiting for transfers between devices: 144 us -> 0 us
  Pallas kernels: 105 us -> 145 us
  between operations: 17.3 us -> 0.68 us
  local copies, waits for them, and re-layouts: 11 us -> 2.69 us
  other arithmetic: 3.79 us -> 0 us
    all_gather x1 -> x0, waiting for transfers between devices: 144 us -> none  [body(): wwin = lax.all_gather(window, 'dp', axis=0)[FIRST:]]
    pallas_call x0 -> x2, Pallas kernels: none -> 43.9 us  [the longest x1 42 us: gather(): pl.pallas_call(gather_kernel, in_specs=[vm], out_specs=vm, out_shape=jax....]
    slice x1 -> x0, local copies, waits for them, and re-layouts: 3.15 us -> none  [body(): wwin = lax.all_gather(window, 'dp', axis=0)[FIRST:]]
    pallas_call x1, Pallas kernels: 49.8 us -> 47 us  [scatter(): pl.pallas_call(scatter_kernel, in_specs=[pl.BlockSpec(memory_space=pltpu....]
  transfers between devices with their start and end apart: 1 -> 0, of which waited for: 1 -> 0; matrix products, arithmetic and copies ran while one was open for 2% -> 0% of each run, Pallas kernels for 0% -> 0%
where the time goes in v2:
time: 149 us
  Pallas kernels  145 us (97%)
  local copies, waits for them, and re-layouts  2.69 us (2%)
    pallas_call x1, Pallas kernels, scatter(): pl.pallas_call(scatter_kernel, in_specs=[pl.BlockSpec(memory_space=pltpu....  47 us
    pallas_call x1, Pallas kernels, gather(): pl.pallas_call(gather_kernel, in_specs=[vm], out_specs=vm, out_shape=jax....  42 us
    pallas_call x1, Pallas kernels, sums(): pl.pallas_call(sums_kernel, in_specs=[vm, vm], out_specs=[vm, vm, vm], ou...  27.6 us
    pallas_call x1, Pallas kernels, grads(): pl.pallas_call(grads_kernel, grid=(PIECES,), in_specs=[whole((RB, 128)),...  24.4 us

profile of v2, /device:TPU:1, one launch (start us, length us, event | category | flops | bytes accessed | tf_op | source)
XLA Modules:
  0.0 148.8 jit_solution(3997425233812095095)
XLA Ops:
  0.6 0.0 copy-start
  0.6 1.9 %prep.1 = (bf16[144,128]{1,0:T(8,128)(2,1)}, f32[8,128]{1,0:T(8,128)}) custom-call(s32[64]{0:T(128)} %lengths.3, bf16[544,128]{1,0:T(8,128)(2,1)} %params.3), custom_call_target="tpu_custom_call" | custom-call | tf_op jit(solution)/shard_map/prep/pallas_call | solution.py:83
  2.5 42.0 %gather.1.wwin = bf16[8,4,3,144,128]{4,3,2,1,0:T(8,128)(2,1)} custom-call(bf16[144,128]{1,0:T(8,128)(2,1)} %get-tuple-element.13.quarter), custom_call_target="tpu_custom_call" | custom-call | tf_op jit(solution)/shard_map/gather/pallas_call | solution.py:180
  44.5 0.0 copy-done
  44.5 0.7 copy.12.up
  45.3 24.4 %grads.1 = bf16[7,256,16,128]{3,2,1,0:T(8,128)(2,1)} custom-call(bf16[80,128]{1,0:T(8,128)(2,1)} %bitcast.9, bf16[80,128]{1,0:T(8,128)(2,1)} %bitcast.8, bf16[128,80]{1,0:T(8,128)(2,1)} %copy.12.up, bf16[8,4,3,144,128]{4,3,2,1,0:T(8,128)(2,1)} %gather.1.wwin, bf16[128,14336]{1,0:T(8,128)(2,1)} %gate.1, bf16[128,14336]{1,0:T(8,128)(2,1)} %upp.1), custom_call_target="tpu_custom_call" | custom-call | tf_op jit(solution)/shard_map/grads/pallas_call | solution.py:244
  69.7 0.0 copy-start.1
  69.7 47.0 %scatter.1.g = f32[112,128]{1,0:T(8,128)} custom-call(bf16[7,2,2,4,16,16,128]{6,5,4,3,2,1,0:T(8,128)(2,1)} %bitcast.6), custom_call_target="tpu_custom_call" | custom-call | tf_op jit(solution)/shard_map/scatter/pallas_call | solution.py:373
  116.7 27.6 %sums.1 = (f32[6,112,128]{2,1,0:T(8,128)}, f32[3,16,8,128]{3,2,1,0:T(8,128)}, f32[3,8,128]{2,1,0:T(8,128)}) custom-call(f32[112,128]{1,0:T(8,128)} %scatter.1.g, f32[8,128]{1,0:T(8,128)} %get-tuple-element.14.wext), custom_call_target="tpu_custom_call" | custom-call | tf_op jit(solution)/shard_map/sums/pallas_call | solution.py:540
  144.3 0.0 copy-done.1
  144.3 0.1 reshape.24
  144.4 0.6 pad.4.row_state
  145.0 2.5 %update.1 = (bf16[544,128]{1,0:T(8,128)(2,1)}, bf16[544,128]{1,0:T(8,128)(2,1)}, f32[3,128]{1,0:T(4,128)}, f32[336,128]{1,0:T(8,128)}) custom-call(s32[64]{0:T(128)} %lengths.3, f32[6,112,128]{2,1,0:T(8,128)} %get-tuple-element.15.gw, f32[3,16,8,128]{3,2,1,0:T(8,128)} %get-tuple-element.16.cols, f32[3,8,128]{2,1,0:T(8,128)} %get-tuple-element.17.extra, ...), custom_call_target="tpu_custom_call" | custom-call | tf_op jit(solution)/shard_map/update/pallas_call | solution.py:607
  147.5 1.3 reshape.26
Async XLA Ops:
  0.6 43.9 %copy-start = (bf16[128,80]{0,1:T(8,128)(2,1)S(1)}, bf16[128,80]{0,1:T(8,128)(2,1)}, u32[]{:S(2)}) copy-start(bf16[128,80]{0,1:T(8,128)(2,1)} %param.9) | copy-start | bytes 61444
  69.7 74.6 %copy-start.1 = (f32[240]{0:T(256)S(1)}, f32[240]{0:T(256)}, u32[]{:S(2)}) copy-start(f32[240]{0:T(256)} %param.14) | copy-start | bytes 2884

commit v3 on v1

v3 whole, which is shorter than its diff:
```python
import functools

import jax
import jax.numpy as jnp
from jax import lax
from jax.experimental import pallas as pl
from jax.experimental.pallas import tpu as pltpu
from jax.sharding import PartitionSpec as P

BETA = 0.8
RHO = 0.2
TINY = 1e-30
RB = 80
NB = 112
EV = 420
JIT = 52
PIECES = 7
WPAD = 1176
WROWS = 10200
BASES = (-1, 3, 7, 10)
COUNTS = (6, 5, 5, 6)
F32 = jnp.float32
BF16 = jnp.bfloat16
VMEM_LIMIT = 60 * 1024 * 1024


def coords():
    r = lax.axis_index("rep")
    p = lax.axis_index("dp")
    x = p // 16
    y = (p // 8 % 2) * 2 + r // 2
    return x, y, p % 8, r % 2


def device(x, y, z, core):
    return {"rep": (y % 2) * 2 + core, "dp": (x * 2 + y // 2) * 8 + z}


def greet(targets):
    barrier = pltpu.get_barrier_semaphore()
    for target in targets:
        pl.semaphore_signal(barrier, inc=1, device_id=target, device_id_type=pl.DeviceIdType.MESH)
    pl.semaphore_wait(barrier, len(targets))


def remote(src, dst, send, recv, target):
    return pltpu.make_async_remote_copy(
        src_ref=src, dst_ref=dst, send_sem=send, recv_sem=recv,
        device_id=target, device_id_type=pl.DeviceIdType.MESH,
    )


def span(lengths):
    p = lax.axis_index("dp")
    start = lax.fori_loop(0, p, lambda k, total: total + lengths[k], jnp.int32(0))
    return start, lengths[p]


def prep_kernel(lengths, params, quarter, wext, shifted):
    p, r = lax.axis_index("dp"), lax.axis_index("rep")
    start, length = span(lengths)
    row = lax.broadcasted_iota(jnp.int32, (544, 128), 0)
    v = jnp.where(row < length, params[...].astype(F32), 0.0)
    shifted[0 : 2 * JIT, :] = jnp.zeros((2 * JIT, 128), F32)
    shifted[2 * JIT : 2 * JIT + 544, :] = v
    shifted[2 * JIT + 544 :, :] = jnp.zeros((72, 128), F32)
    at = 2 * JIT - (start - (EV * p - JIT)) + 144 * r
    quarter[...] = shifted[pl.ds(at, 144), :].astype(BF16)
    v = v * v
    flat = row + start
    lane = lax.broadcasted_iota(jnp.int32, (8, 128), 1)
    total = jnp.zeros((8, 128), F32)
    for m in range(3):
        inside = (flat >= m * 8960) & (flat < m * 8960 + 8960)
        total += jnp.where(lane == 120 + m, 0.25 * jnp.sum(jnp.where(inside, v, 0.0)), 0.0)
    wext[...] = total


def prep(shard_rows, params):
    vm = pl.BlockSpec(memory_space=pltpu.VMEM)
    return pl.pallas_call(
        prep_kernel,
        in_specs=[pl.BlockSpec(memory_space=pltpu.SMEM), vm],
        out_specs=[vm, vm],
        out_shape=[jax.ShapeDtypeStruct((144, 128), BF16), jax.ShapeDtypeStruct((8, 128), F32)],
        scratch_shapes=[pltpu.VMEM((720, 128), F32)],
        compiler_params=pltpu.CompilerParams(vmem_limit_bytes=VMEM_LIMIT),
        name="prep",
    )(shard_rows, params)


def matrix_of(n):
    return jnp.where(n < 4, 2, jnp.where(n < 9, 0, jnp.where(n < 14, 1, 2)))


def index_of(n):
    return jnp.where(n < 4, n, jnp.where(n < 9, n - 4, jnp.where(n < 14, n - 9, 4)))


def member(z, core):
    return z % 4 * 4 + z // 4 * 2 + core


def main_kernel(
    tok_t, up_t, gate_hbm, upp_hbm, quarter, wext, gw, cols, extra,
    gate, upp, act, fac, w, wflat, rows, fa, fb, c1a, c1b, a1a, a1b, c2a, c2b, a2a, a2b, own2a, own2b,
    c3a, c3b, a3, c4, up, g, sq, pa, acc, pb, tot, pc,
    sg, su, w1, v1, wp, vp, wm, vm, wy, vy, wc, vc,
    s1, r1, s2, r2, s3, r3, s4, r4, ssa, rsa, ssb, rsb, ssc, rsc, ssd, rsd, ssg, rsg,
):
    x, y, z, core = coords()
    r, p = lax.axis_index("rep"), lax.axis_index("dp")
    plane = p // 8
    other = device(x, y, z, 1 - core)
    along_x = lambda d: device((x + d) % 4, y, z, core)
    along_y = lambda d: device(x, (y + d) % 4, z, core)
    along_z = lambda d: device(x, y, (z + d) % 8, core)

    def load(c):
        part = pl.ds(pl.multiple_of(c * 2048, 2048), 2048)
        return (
            pltpu.make_async_copy(gate_hbm.at[:, part], gate.at[c], sg.at[c]),
            pltpu.make_async_copy(upp_hbm.at[:, part], upp.at[c], su.at[c]),
        )

    def begin(c, carry):
        for copy in load(c):
            copy.start()
        return carry

    lax.fori_loop(0, PIECES, begin, 0)
    greet(
        [other]
        + [along_x(d) for d in (1, 2, 3)]
        + [along_y(d) for d in (1, 2, 3)]
        + [along_z(d) for d in range(1, 8)]
        + [device((x + d) % 4, (y + 2) % 4, z, core) for d in (1, 2, 3)]
    )

    spread = lambda d: {"rep": r, "dp": (plane + d) % 8 * 8 + z}
    mate = (1 - r // 2) * 2 + core

    def copy_spread(d):
        return remote(quarter, w.at[z, r, jnp.maximum(plane - 5, 0)], w1.at[d - 1], v1.at[jnp.maximum(plane - 5, 0)], spread(d))

    def copy_up(s, u):
        block = w.at[(z + 9 - s) % 8, r, u]
        n = (s - 1) * 3 + u
        return remote(block, block, wp.at[n], vp.at[n], along_z(1))

    def copy_down(s, u):
        block = w.at[(z + s - 1) % 8, r, u]
        n = (s - 1) * 3 + u
        return remote(block, block, wm.at[n], vm.at[n], along_z(7))

    def copy_y(k, u):
        block = w.at[(z + 8 - k) % 8, r, u]
        to = jnp.where((k == 0) | (k > 4), 3, 1)
        return remote(block, block, wy.at[k * 3 + u], vy.at[k * 3 + u], along_y(to))

    def copy_core(k, q, u):
        block = w.at[(z + 8 - k) % 8, q, u]
        n = (jnp.where(q == r, 0, 8) + k) * 3 + u
        return remote(block, block, wc.at[n], vc.at[n], other)

    @pl.when(p >= 40)
    def _():
        for d in range(1, 8):
            copy_spread(d).start()
        w[z, r, jnp.maximum(plane - 5, 0)] = quarter[...]

    def gather_first():
        for u in range(3):
            @pl.when(plane != 5 + u)
            def _():
                remote(quarter, w.at[z, r, u], w1.at[0], v1.at[u], spread(1)).wait_recv()
            copy_up(1, u).start()
            copy_down(1, u).start()
            copy_y(0, u).start()
            copy_core(0, r, u).start()

    def gather_ring(s):
        for u in range(3):
            copy_up(s, u).wait_recv()
            if s < 4:
                copy_up(s + 1, u).start()
            copy_y(s, u).start()
            copy_core(s, r, u).start()
            if s < 4:
                copy_down(s, u).wait_recv()
                if s < 3:
                    copy_down(s + 1, u).start()
                copy_y(8 - s, u).start()
                copy_core(8 - s, r, u).start()

    f, c1, a1, c2 = (fa, fb), (c1a, c1b), (a1a, a1b), (c2a, c2b)
    a2, own2, c3 = (a2a, a2b), (own2a, own2b), (c3a, c3b)
    first, second = (x, y), (y, x)
    axis_of = (along_x, along_y)

    def copy1(t, c):
        k = t * PIECES + c
        return remote(f[t].at[c, 1 - core], c1[t].at[c], s1.at[k], r1.at[k], other)

    def copy2(t, c, h, d):
        k, n = t * PIECES + c, h * 3 + d - 1
        return remote(a1[t].at[c, h, (first[h] + d) % 4], c2[t].at[c, h, d - 1], s2.at[k, n], r2.at[k, n], axis_of[h](d))

    def copy3(t, c, h, d):
        k, n = t * PIECES + c, h * 3 + d - 1
        return remote(a2[t].at[c, h, (second[h] + d) % 4], c3[t].at[c, h, d - 1], s3.at[k, n], r3.at[k, n], axis_of[1 - h](d))

    def copy4(c, d):
        to = (z + d) % 8
        return remote(a3.at[c, to // 4, to % 4], c4.at[c, d - 1], s4.at[c, d - 1], r4.at[c, d - 1], along_z(d))

    def step1(t, c):
        copy1(t, c).wait_recv()
        for h in range(2):
            def add(i, carry):
                a1[t][c, h, i] = (f[t][c, core, h, i].astype(F32) + c1[t][c, h, i].astype(F32)).astype(BF16)
                return carry
            lax.fori_loop(0, 4, add, 0)
            for d in (1, 2, 3):
                copy2(t, c, h, d).start()

    def step2(t, c):
        nz = (1, 3)[t]
        for h in range(2):
            for d in (1, 2, 3):
                copy2(t, c, h, d).wait_recv()
            def add(i, carry):
                part = pl.ds(i * nz, nz)
                v = f[t][c, core, h, first[h], part].astype(F32) + c1[t][c, h, first[h], part].astype(F32)
                for d in range(3):
                    v += c2[t][c, h, d, part].astype(F32)
                a2[t][c, h, i] = v.astype(BF16)
                own2[t][i] = v
                return carry
            lax.fori_loop(0, 4, add, 0)
            a3[c, h, pl.ds(t, nz)] = own2[t][second[h]]
            for d in (1, 2, 3):
                copy3(t, c, h, d).start()

    def step3(t, c):
        nz = (1, 3)[t]
        for h in range(2):
            for d in (1, 2, 3):
                copy3(t, c, h, d).wait_recv()
            v = a3[c, h, pl.ds(t, nz)]
            for d in range(3):
                v += c3[t][c, h, d].astype(F32)
            a3[c, h, pl.ds(t, nz)] = v

    def put(n, big, c, v):
        core_of, h, zz = n % 2, n // 2 % 2, n // 4
        one, two = (big // 4, big % 4) if h == 0 else (big % 4, big // 4)
        if zz == 0:
            fa[c, core_of, h, one, two] = v
        else:
            fb[c, core_of, h, one, two * 3 + zz - 1] = v

    wflat[...] = jnp.zeros_like(wflat)
    up[...] = up_t[...].astype(F32).T.astype(BF16)
    def clear(c, carry):
        def one(i, carry):
            for j in range(4):
                fb[c, 1, 1, i, j * 3 + 2] = jnp.zeros((16, 128), BF16)
            return carry
        return lax.fori_loop(0, 4, one, carry)
    lax.fori_loop(0, PIECES, clear, 0)

    def phase_a(c, carry):
        for copy in load(c):
            copy.wait()
        def block(jj, carry):
            here = pl.ds(pl.multiple_of(jj * 256, 256), 256)
            there = pl.ds(pl.multiple_of(c * 2048 + jj * 256, 256), 256)
            gv = gate[c, :, here].astype(F32)
            uv = upp[c, :, here].astype(F32)
            s = 0.5 * jnp.tanh(0.5 * gv) + 0.5
            av = gv * s
            act[:, there] = av
            fac[:, there] = uv * s * (1.0 + gv * (1.0 - s))
            gd = jnp.dot(up_t[...], (av * uv).astype(BF16), preferred_element_type=F32)
            for b in range(2):
                rows[pl.ds(jj * 2 + b, RB, stride=16), :] = gd[:, b * 128 : b * 128 + 128]
            return carry
        lax.fori_loop(0, 8, block, 0, unroll=4)
        def pack(big, carry):
            for idx in range(5):
                at = pl.ds(pl.multiple_of((big * 5 + idx) * 16, 16), 16)
                put(idx if idx < 4 else 14, big, c, rows[at, :].astype(BF16))
            return carry
        lax.fori_loop(0, 16, pack, 0, unroll=2)
        copy1(0, c).start()
        @pl.when(c > 0)
        def _():
            step1(0, c - 1)
        for at, what in ((3, gather_first), (5, lambda: gather_ring(1))):
            @pl.when(c == at)
            def _():
                what()
        return carry

    lax.fori_loop(0, PIECES, phase_a, 0)
    step1(0, PIECES - 1)
    for s in (2, 3, 4):
        gather_ring(s)

    def build(j, carry):
        k = jnp.where(j % 2 == 1, (j + 1) // 2, (8 - j // 2) % 8)
        o = (z + 8 - k) % 8
        for u in range(3):
            copy_y(k, u).wait_recv()
            copy_core(k, mate, u).start()
        for u in range(3):
            copy_core(k, r, u).wait_recv()
            copy_core(k, mate, u).wait_recv()
        for u in range(3):
            off = EV * (8 * u + o) + 4
            for q in range(4):
                for t in range(9 if q < 3 else 6):
                    v = w[o, q, u, t * 16 : t * 16 + 16, :].astype(F32)
                    for half in range(2):
                        at = q * 144 + t * 16 + half * 8
                        if 2 * JIT <= at < 416:
                            wflat[pl.ds(off + at, 8), :] = v[half * 8 : half * 8 + 8]
                        else:
                            wflat[pl.ds(off + at, 8), :] += v[half * 8 : half * 8 + 8]
        return carry

    lax.fori_loop(0, 8, build, 0)

    def phase_b(c, carry):
        def block(jj, carry):
            there = pl.ds(pl.multiple_of(c * 2048 + jj * 256, 256), 256)
            j = c * 16 + jj * 2
            wv = jnp.concatenate(
                [wflat[pl.ds(WPAD + j + b, RB, stride=NB), :] for b in range(2)], axis=1
            ).astype(BF16)
            dh = jnp.dot(up[...], wv, preferred_element_type=F32)
            gg = jnp.dot(tok_t[...], (dh * fac[:, there]).astype(BF16), preferred_element_type=F32)
            gu = jnp.dot(tok_t[...], (dh * act[:, there]).astype(BF16), preferred_element_type=F32)
            for m, v in enumerate((gg, gu)):
                for b in range(2):
                    rows[pl.ds(m * RB * 16 + jj * 2 + b, RB, stride=16), :] = v[:, b * 128 : b * 128 + 128]
            return carry
        lax.fori_loop(0, 8, block, 0, unroll=4)
        def pack(big, carry):
            for n in range(4, 14):
                row = (n - 4) // 5 * RB + (n - 4) % 5
                at = pl.ds(pl.multiple_of((big * 5 + row) * 16, 16), 16)
                put(n, big, c, rows[at, :].astype(BF16))
            return carry
        lax.fori_loop(0, 16, pack, 0, unroll=2)
        copy1(1, c).start()
        step2(0, c)
        @pl.when(c > 0)
        def _():
            step1(1, c - 1)
            step3(0, c - 1)
        return carry

    lax.fori_loop(0, PIECES, phase_b, 0)
    step1(1, PIECES - 1)
    step3(0, PIECES - 1)

    def loop2(c, carry):
        step2(1, c)
        return carry

    def loop3(c, carry):
        step3(1, c)
        for d in range(1, 8):
            copy4(c, d).start()
        return carry

    def loop4(c, carry):
        for d in range(1, 8):
            copy4(c, d).wait_recv()
        v = a3[c, z // 4, z % 4]
        for d in range(7):
            v += c4[c, d]
        g[pl.ds(pl.multiple_of(c * 16, 16), 16), :] = v * (1.0 / 32768.0)
        return carry

    for loop in (loop2, loop3, loop4):
        lax.fori_loop(0, PIECES, loop, 0)

    n_own = member(z, core)
    real = n_own < 15
    own_m = matrix_of(n_own)
    i_own = (x * 4 + y) * 5 + index_of(n_own)
    row = own_m * RB + i_own
    ka, kb = z * 2 + core, x * 4 + y
    in_a = lambda d: (lambda k: device(x, y, k // 2, k % 2))((ka + d) % 16)
    in_b = lambda d: (lambda k: device(k // 4, k % 4, z, core))((kb + d) % 16)

    squares = g[...] * g[...]
    lane = lax.broadcasted_iota(jnp.int32, (1, 128), 1)
    last = jnp.where((lane == i_own) & real, jnp.sum(squares), 0.0) + wext[0:1, :]
    for k in range(16):
        sq[k, 0:7, :] = squares[7 * k : 7 * k + 7, :]
        sq[k, 7:8, :] = last

    def copy_a(d):
        return remote(sq.at[(ka + d) % 16], pa.at[d - 1], ssa.at[d - 1], rsa.at[d - 1], in_a(d))

    def copy_b(d):
        return remote(acc, pb.at[d - 1], ssb.at[d - 1], rsb.at[d - 1], in_b(d))

    def copy_c(d):
        return remote(pc.at[0, z], pc.at[0, z], ssc.at[d - 1], rsc.at[d - 1], along_z(d))

    def copy_d(d):
        return remote(pc.at[0, (z + 8 - d) % 8], pc.at[1, (z + 8 - d) % 8], ssd.at[d], rsd.at[d], other)

    for d in range(1, 16):
        copy_a(d).start()

    gv, qv = row // 15, row % 15

    def give(fn):
        for t in range(6):
            if t < 4:
                owner, k = 4 * gv + t, qv - BASES[t]
                ok = (k >= 0) & (k < COUNTS[t]) & real
                k = jnp.clip(k, 0, 5)
            elif t == 4:
                owner, k, ok = jnp.maximum(4 * gv - 1, 0), 5, (qv == 0) & (gv > 0) & real
            else:
                owner, k, ok = jnp.minimum(4 * gv + 4, 63), 0, (qv == 14) & (gv < 15) & real
            for rr in range(4):
                fn(owner, k, ok, rr, t * 4 + rr)

    def send_row(owner, k, ok, rr, n):
        @pl.when(ok & ((owner != p) | (rr != r)))
        def _():
            remote(g, gw.at[k], ssg.at[n], rsg.at[k], {"rep": rr, "dp": owner}).start()
        @pl.when(ok & (owner == p) & (rr == r))
        def _():
            gw[k] = g[...]

    give(send_row)

    def source(k):
        return matrix_of(member(k // 2, k % 2))

    v = sq[ka]
    for m in range(3):
        acc[m] = jnp.where(own_m == m, v, 0.0)
    for d in range(1, 16):
        copy_a(d).wait_recv()
        v = pa[d - 1]
        m_src = source((ka + 16 - d) % 16)
        for m in range(3):
            acc[m] += jnp.where(m_src == m, v, 0.0)
    for d in range(1, 16):
        copy_b(d).start()
    tot[...] = acc[...]
    for d in range(1, 16):
        copy_b(d).wait_recv()
        tot[...] += pb[d - 1]
    pc[0, z] = tot[...]
    for d in (4, 3, 5, 2, 6, 1, 7):
        copy_c(d).start()
    copy_d(0).start()
    extra[...] = tot[...]
    for d in (1, 7, 2, 6, 3, 5, 4):
        copy_c(d).wait_recv()
        copy_d(d).start()
    for d in range(8):
        copy_d(d).wait_recv()
    for k in range(8):
        for m in range(3):
            cols[m, 2 * k + core] = pc[0, k, m]
            cols[m, 2 * k + 1 - core] = pc[1, k, m]

    a = p % 4
    base = 15 * (p // 4) + jnp.where(a == 0, -1, jnp.where(a == 1, 3, jnp.where(a == 2, 7, 10)))
    for k in range(6):
        if k == 0:
            ok = p > 0
        elif k == 5:
            ok = (a == 0) | ((a == 3) & (p < 63))
        else:
            ok = p >= 0
        @pl.when(ok & ((base + k != row) | jnp.logical_not(real)))
        def _():
            remote(g, gw.at[k], ssg.at[k], rsg.at[k], other).wait_recv()
        @pl.when(jnp.logical_not(ok))
        def _():
            gw[k] = jnp.zeros((NB, 128), F32)

    def wait_row(owner, k, ok, rr, n):
        @pl.when(ok & ((owner != p) | (rr != r)))
        def _():
            remote(g, gw.at[k], ssg.at[n], rsg.at[k], {"rep": rr, "dp": owner}).wait_send()

    give(wait_row)
    for d in range(1, 16):
        copy_a(d).wait_send()
        copy_b(d).wait_send()
    for d in range(8):
        if d:
            copy_c(d).wait_send()
        copy_d(d).wait_send()

    @pl.when(p >= 40)
    def _():
        for d in range(1, 8):
            copy_spread(d).wait_send()

    for u in range(3):
        for s in range(1, 5):
            copy_up(s, u).wait_send()
            if s < 4:
                copy_down(s, u).wait_send()

    def drain_w(k, carry):
        for u in range(3):
            copy_y(k, u).wait_send()
            copy_core(k, r, u).wait_send()
            copy_core(k, mate, u).wait_send()
        return carry

    def drain(c, carry):
        for t in range(2):
            copy1(t, c).wait_send()
            for h in range(2):
                for d in (1, 2, 3):
                    copy2(t, c, h, d).wait_send()
                    copy3(t, c, h, d).wait_send()
        for d in range(1, 8):
            copy4(c, d).wait_send()
        return carry

    lax.fori_loop(0, 8, drain_w, 0)
    lax.fori_loop(0, PIECES, drain, 0)


def main(tokens, upstream, gate_pre, up_pre, quarter, wext):
    n = PIECES
    dma = lambda *shape: pltpu.SemaphoreType.DMA(shape)
    vm = pl.BlockSpec(memory_space=pltpu.VMEM)
    hbm = pl.BlockSpec(memory_space=pl.ANY)
    both = lambda *shape: [pltpu.VMEM(shape[:-1] + (k * shape[-1], 16, 128), BF16) for k in (1, 3)]
    return pl.pallas_call(
        main_kernel,
        in_specs=[vm, vm, hbm, hbm, vm, vm],
        out_specs=[vm, vm, vm],
        out_shape=[
            jax.ShapeDtypeStruct((6, NB, 128), F32),
            jax.ShapeDtypeStruct((3, 16, 8, 128), F32),
            jax.ShapeDtypeStruct((3, 8, 128), F32),
        ],
        scratch_shapes=[
            pltpu.VMEM((n, 128, 2048), BF16),
            pltpu.VMEM((n, 128, 2048), BF16),
            pltpu.VMEM((128, 14336), F32),
            pltpu.VMEM((128, 14336), F32),
            pltpu.VMEM((8, 4, 3, 144, 128), BF16),
            pltpu.VMEM((WROWS, 128), F32),
            pltpu.VMEM((2 * RB * 16, 128), F32),
            *both(n, 2, 2, 4, 4),
            *both(n, 2, 4, 4),
            *both(n, 2, 4, 4),
            *both(n, 2, 3, 4),
            *both(n, 2, 4, 1),
            pltpu.VMEM((4, 1, 16, 128), F32),
            pltpu.VMEM((4, 3, 16, 128), F32),
            *both(n, 2, 3, 1),
            pltpu.VMEM((n, 2, 4, 16, 128), F32),
            pltpu.VMEM((n, 7, 16, 128), F32),
            pltpu.VMEM((128, RB), BF16),
            pltpu.VMEM((NB, 128), F32),
            pltpu.VMEM((16, 8, 128), F32),
            pltpu.VMEM((15, 8, 128), F32),
            pltpu.VMEM((3, 8, 128), F32),
            pltpu.VMEM((15, 3, 8, 128), F32),
            pltpu.VMEM((3, 8, 128), F32),
            pltpu.VMEM((2, 8, 3, 8, 128), F32),
            dma(n), dma(n),
            dma(7), dma(3), dma(12), dma(12), dma(9), dma(9), dma(24), dma(24), dma(48), dma(48),
            dma(2 * n), dma(2 * n), dma(2 * n, 6), dma(2 * n, 6), dma(2 * n, 6), dma(2 * n, 6), dma(n, 7), dma(n, 7),
            dma(15), dma(15), dma(15), dma(15), dma(7), dma(7), dma(8), dma(8), dma(24), dma(6),
        ],
        compiler_params=pltpu.CompilerParams(
            vmem_limit_bytes=VMEM_LIMIT, collective_id=0, has_side_effects=True
        ),
        name="main",
    )(tokens.T, upstream.T, gate_pre, up_pre, quarter, wext)


def update_kernel(lengths, gw, cols, extra, params, row_state, col_state, out_p, out_d, out_r, out_c, moved, scaled):
    p = lax.axis_index("dp")
    start, length = span(lengths)
    a = p % 4
    first = 15 * (p // 4) + jnp.where(a == 0, -1, jnp.where(a == 1, 3, jnp.where(a == 2, 7, 10)))
    shift = start - NB * first
    for m in range(3):
        for k in range(16):
            part = pl.ds(m * NB + 7 * k, 7)
            out_c[part, :] = BETA * col_state[part, :] + (1.0 - BETA) * (cols[m, k, 0:7, :] * (1.0 / RB) + TINY)
    lane = lax.broadcasted_iota(jnp.int32, (1, 128), 1)
    sums_row = extra[:, 7, :]
    live = lax.broadcasted_iota(jnp.int32, (3, 128), 1) < RB
    rows = jnp.where(live, BETA * row_state[...] + (1.0 - BETA) * (sums_row * (1.0 / 14336.0) + TINY), 0.0)
    out_r[...] = rows
    means = jnp.sum(rows, axis=1, keepdims=True) * (1.0 / RB)
    weight = jnp.sum(sums_row, axis=0, keepdims=True)
    for k in range(6):
        row = jnp.clip(first + k, 0, 239)
        m = row // RB
        i = row % RB
        pick = lambda v: jnp.where(m == 0, v[0:1], jnp.where(m == 1, v[1:2], v[2:3]))
        value = jnp.sum(jnp.where(lane == i, pick(rows), 0.0), axis=1, keepdims=True)
        sq = jnp.sum(jnp.where(lane == 120 + m, weight, 0.0), axis=1, keepdims=True)
        scale = RHO * jnp.sqrt(sq * (1.0 / (RB * 14336.0)))
        factor = value / pick(means)
        v = gw[k] * lax.rsqrt(factor * out_c[pl.ds(pl.multiple_of(m * NB, 8), NB), :])
        moved[pl.ds(k * NB, NB), :] = v
        scaled[pl.ds(k * NB, NB), :] = scale * v
    def tile(t, carry):
        o = pl.multiple_of(t * 16, 16)
        at = pl.ds(shift + o, 16)
        keep = o + lax.broadcasted_iota(jnp.int32, (16, 128), 0) < length
        out_d[pl.ds(o, 16), :] = jnp.where(keep, moved[at, :], 0.0).astype(BF16)
        new = params[pl.ds(o, 16), :].astype(F32) - scaled[at, :]
        out_p[pl.ds(o, 16), :] = jnp.where(keep, new, 0.0).astype(BF16)
        return carry
    lax.fori_loop(0, 34, tile, 0)


def update(lengths, gw, cols, extra, params, row_state, col_state):
    vm = pl.BlockSpec(memory_space=pltpu.VMEM)
    return pl.pallas_call(
        update_kernel,
        in_specs=[pl.BlockSpec(memory_space=pltpu.SMEM)] + [vm] * 6,
        out_specs=[vm] * 4,
        out_shape=[
            jax.ShapeDtypeStruct((544, 128), BF16),
            jax.ShapeDtypeStruct((544, 128), BF16),
            jax.ShapeDtypeStruct((3, 128), F32),
            jax.ShapeDtypeStruct((336, 128), F32),
        ],
        scratch_shapes=[pltpu.VMEM((800, 128), F32), pltpu.VMEM((800, 128), F32)],
        compiler_params=pltpu.CompilerParams(vmem_limit_bytes=VMEM_LIMIT),
        name="update",
    )(lengths, gw, cols, extra, params, row_state, col_state)


def body(tokens, upstream, gate_pre, up_pre, param_shards, shard_rows, row_state, col_state):
    quarter, wext = prep(shard_rows, param_shards)
    gw, cols, extra = main(tokens, upstream, gate_pre, up_pre, quarter, wext)
    row_in = jnp.pad(row_state.reshape(3, RB), ((0, 0), (0, 128 - RB)))
    new_params, direction, rows, new_cols = update(
        shard_rows, gw, cols, extra, param_shards, row_in, col_state.reshape(336, 128)
    )
    return (new_params, direction, rows[:, :RB].reshape(-1), new_cols.reshape(-1))


def solution(mesh):
    in_specs = (
        P(("rep", "dp"), None),
        P(("rep", "dp"), None),
        P(("rep", "dp"), None),
        P(("rep", "dp"), None),
        P("dp", None),
        P(),
        P(),
        P(),
    )
    out_specs = (P("dp", None), P("dp", None), P(), P())
    return jax.shard_map(body, mesh=mesh, in_specs=in_specs, out_specs=out_specs, check_vma=False)
```

time: 281 us -> 121 us (0.43)
  waiting for transfers between devices: 144 us -> 0 us
  between operations: 17.3 us -> 0.64 us
  Pallas kernels: 105 us -> 117 us
  local copies, waits for them, and re-layouts: 11 us -> 2.67 us
  other arithmetic: 3.79 us -> 0 us
    all_gather x1 -> x0, waiting for transfers between devices: 144 us -> none  [body(): wwin = lax.all_gather(window, 'dp', axis=0)[FIRST:]]
    pallas_call x3 -> x2, Pallas kernels: 102 us -> 115 us  [the longest x1 113 us: main(): pl.pallas_call(main_kernel, in_specs=[vm, vm, hbm, hbm, vm, vm], out_spec...]
    slice x1 -> x0, local copies, waits for them, and re-layouts: 3.15 us -> none  [body(): wwin = lax.all_gather(window, 'dp', axis=0)[FIRST:]]
  transfers between devices with their start and end apart: 1 -> 0, of which waited for: 1 -> 0; matrix products, arithmetic and copies ran while one was open for 2% -> 0% of each run, Pallas kernels for 0% -> 0%
where the time goes in v3:
time: 121 us
  Pallas kernels  117 us (97%)
  local copies, waits for them, and re-layouts  2.67 us (2%)
    pallas_call x1, Pallas kernels, main(): pl.pallas_call(main_kernel, in_specs=[vm, vm, hbm, hbm, vm, vm], out_spec...  113 us
    pallas_call x1, Pallas kernels, update(): pl.pallas_call(update_kernel, in_specs=[pl.BlockSpec(memory_space=pltpu.S...  2.5 us

profile of v3, /device:TPU:1, one launch (start us, length us, event | category | flops | bytes accessed | tf_op | source)
XLA Modules:
  0.0 120.8 jit_solution(12597603240310093426)
XLA Ops:
  0.6 0.8 reshape.20
  1.4 0.6 pad.4.row_state
  2.0 1.9 %prep.1 = (bf16[144,128]{1,0:T(8,128)(2,1)}, f32[8,128]{1,0:T(8,128)}) custom-call(s32[64]{0:T(128)} %lengths.3, bf16[544,128]{1,0:T(8,128)(2,1)} %params.3), custom_call_target="tpu_custom_call" | custom-call | tf_op jit(solution)/shard_map/prep/pallas_call | solution.py:81
  3.9 113.1 %main.1 = (f32[6,112,128]{2,1,0:T(8,128)}, f32[3,16,8,128]{3,2,1,0:T(8,128)}, f32[3,8,128]{2,1,0:T(8,128)}) custom-call(bf16[80,128]{1,0:T(8,128)(2,1)} %bitcast.6, bf16[80,128]{1,0:T(8,128)(2,1)} %bitcast.7, bf16[128,14336]{1,0:T(8,128)(2,1)} %gate_hbm.1, bf16[128,14336]{1,0:T(8,128)(2,1)} %upp_hbm.1, bf16[144,128]{1,0:T(8,128)(2,1)} %get-tuple-element.13.quarter, ...), custom_call_target="tpu_custom_call" | custom-call | tf_op jit(solution)/shard_map/main/pallas_call | solution.py:549
  117.0 2.5 %update.1 = (bf16[544,128]{1,0:T(8,128)(2,1)}, bf16[544,128]{1,0:T(8,128)(2,1)}, f32[3,128]{1,0:T(4,128)}, f32[336,128]{1,0:T(8,128)}) custom-call(s32[64]{0:T(128)} %lengths.3, f32[6,112,128]{2,1,0:T(8,128)} %get-tuple-element.15.gw, f32[3,16,8,128]{3,2,1,0:T(8,128)} %get-tuple-element.16.cols, f32[3,8,128]{2,1,0:T(8,128)} %get-tuple-element.17.extra, ...), custom_call_target="tpu_custom_call" | custom-call | tf_op jit(solution)/shard_map/update/pallas_call | solution.py:638
  119.5 1.3 %reshape.22 = f32[240]{0:T(256)} reshape(f32[3,80]{1,0:T(4,128)} %bitcast.8) | data formatting | bytes 1920 | tf_op jit(solution)/shard_map/reshape | solution.py:661

commit v4 on v3

--- a/solution.py
+++ b/solution.py
@@ -36,11 +36,10 @@
     return {"rep": (y % 2) * 2 + core, "dp": (x * 2 + y // 2) * 8 + z}
 
 
-def greet(targets):
+def hello(targets):
     barrier = pltpu.get_barrier_semaphore()
     for target in targets:
         pl.semaphore_signal(barrier, inc=1, device_id=target, device_id_type=pl.DeviceIdType.MESH)
-    pl.semaphore_wait(barrier, len(targets))
 
 
 def remote(src, dst, send, recv, target):
@@ -52,7 +51,8 @@
 
 def span(lengths):
     p = lax.axis_index("dp")
-    start = lax.fori_loop(0, p, lambda k, total: total + lengths[k], jnp.int32(0))
+    add = lambda k, total: total + jnp.where(k < p, lengths[k], 0)
+    start = lax.fori_loop(0, 64, add, jnp.int32(0), unroll=8)
     return start, lengths[p]
 
 
@@ -64,7 +64,7 @@
     shifted[0 : 2 * JIT, :] = jnp.zeros((2 * JIT, 128), F32)
     shifted[2 * JIT : 2 * JIT + 544, :] = v
     shifted[2 * JIT + 544 :, :] = jnp.zeros((72, 128), F32)
-    at = 2 * JIT - (start - (EV * p - JIT)) + 144 * r
+    at = jnp.clip(2 * JIT - (start - (EV * p - JIT)) + 144 * r, 0, 576)
     quarter[...] = shifted[pl.ds(at, 144), :].astype(BF16)
     v = v * v
     flat = row + start
@@ -104,9 +104,9 @@
 def main_kernel(
     tok_t, up_t, gate_hbm, upp_hbm, quarter, wext, gw, cols, extra,
     gate, upp, act, fac, w, wflat, rows, fa, fb, c1a, c1b, a1a, a1b, c2a, c2b, a2a, a2b, own2a, own2b,
-    c3a, c3b, a3, c4, up, g, sq, pa, acc, pb, tot, pc,
+    c3a, c3b, a3, c4, up, g, gb, sq, pa, acc, pb, tot, pc,
     sg, su, w1, v1, wp, vp, wm, vm, wy, vy, wc, vc,
-    s1, r1, s2, r2, s3, r3, s4, r4, ssa, rsa, ssb, rsb, ssc, rsc, ssd, rsd, ssg, rsg,
+    s1, r1, s2, r2, s3, r3, s4, r4, ssa, rsa, ssb, rsb, ssc, rsc, ssd, rsd, ssg, rsg, ssf, rsf,
 ):
     x, y, z, core = coords()
     r, p = lax.axis_index("rep"), lax.axis_index("dp")
@@ -129,13 +129,14 @@
         return carry
 
     lax.fori_loop(0, PIECES, begin, 0)
-    greet(
+    hello(
         [other]
         + [along_x(d) for d in (1, 2, 3)]
         + [along_y(d) for d in (1, 2, 3)]
         + [along_z(d) for d in range(1, 8)]
         + [device((x + d) % 4, (y + 2) % 4, z, core) for d in (1, 2, 3)]
     )
+    pl.semaphore_wait(pltpu.get_barrier_semaphore(), 17)
 
     spread = lambda d: {"rep": r, "dp": (plane + d) % 8 * 8 + z}
     mate = (1 - r // 2) * 2 + core
@@ -297,7 +298,7 @@
         @pl.when(c > 0)
         def _():
             step1(0, c - 1)
-        for at, what in ((3, gather_first), (5, lambda: gather_ring(1))):
+        for at, what in ((2, gather_first), (3, lambda: gather_ring(1)), (5, lambda: gather_ring(2))):
             @pl.when(c == at)
             def _():
                 what()
@@ -305,8 +306,12 @@
 
     lax.fori_loop(0, PIECES, phase_a, 0)
     step1(0, PIECES - 1)
-    for s in (2, 3, 4):
-        gather_ring(s)
+    gather_ring(3)
+    for c in range(4):
+        step2(0, c)
+    gather_ring(4)
+    for c in range(4, PIECES):
+        step2(0, c)
 
     def build(j, carry):
         k = jnp.where(j % 2 == 1, (j + 1) // 2, (8 - j // 2) % 8)
@@ -355,26 +360,30 @@
             return carry
         lax.fori_loop(0, 16, pack, 0, unroll=2)
         copy1(1, c).start()
-        step2(0, c)
+        step3(0, c)
         @pl.when(c > 0)
         def _():
             step1(1, c - 1)
-            step3(0, c - 1)
+        @pl.when(c > 2)
+        def _():
+            step2(1, c - 3)
+        @pl.when(c > 3)
+        def _():
+            last_two(c - 4)
         return carry
 
-    lax.fori_loop(0, PIECES, phase_b, 0)
-    step1(1, PIECES - 1)
-    step3(0, PIECES - 1)
-
-    def loop2(c, carry):
-        step2(1, c)
-        return carry
-
-    def loop3(c, carry):
+    def last_two(c):
         step3(1, c)
         for d in range(1, 8):
             copy4(c, d).start()
-        return carry
+
+    lax.fori_loop(0, PIECES, phase_b, 0)
+    step1(1, PIECES - 1)
+
+    for c in range(PIECES - 3, PIECES):
+        step2(1, c)
+        last_two(c - 1)
+    last_two(PIECES - 1)
 
     def loop4(c, carry):
         for d in range(1, 8):
@@ -385,8 +394,7 @@
         g[pl.ds(pl.multiple_of(c * 16, 16), 16), :] = v * (1.0 / 32768.0)
         return carry
 
-    for loop in (loop2, loop3, loop4):
-        lax.fori_loop(0, PIECES, loop, 0)
+    lax.fori_loop(0, PIECES, loop4, 0)
 
     n_own = member(z, core)
     real = n_own < 15
@@ -431,18 +439,52 @@
                 owner, k, ok = jnp.maximum(4 * gv - 1, 0), 5, (qv == 0) & (gv > 0) & real
             else:
                 owner, k, ok = jnp.minimum(4 * gv + 4, 63), 0, (qv == 14) & (gv < 15) & real
-            for rr in range(4):
-                fn(owner, k, ok, rr, t * 4 + rr)
+            for half in range(2):
+                fn(owner, k, ok, 2 * half + core, t * 2 + half)
 
     def send_row(owner, k, ok, rr, n):
         @pl.when(ok & ((owner != p) | (rr != r)))
         def _():
-            remote(g, gw.at[k], ssg.at[n], rsg.at[k], {"rep": rr, "dp": owner}).start()
+            remote(gb, gw.at[k], ssg.at[n], rsg.at[k], {"rep": rr, "dp": owner}).start()
         @pl.when(ok & (owner == p) & (rr == r))
         def _():
-            gw[k] = g[...]
-
+            gw[k] = gb[...]
+
+    gb[...] = g[...].astype(BF16)
     give(send_row)
+
+    a = p % 4
+    base = 15 * (p // 4) + jnp.where(a == 0, -1, jnp.where(a == 1, 3, jnp.where(a == 2, 7, 10)))
+
+    def window(arriving):
+        for k in range(6):
+            if k == 0:
+                ok = p > 0
+            elif k == 5:
+                ok = (a == 0) | ((a == 3) & (p < 63))
+            else:
+                ok = p >= 0
+            at = jnp.clip(base + k, 0, 239)
+            m, idx = at // RB, at % 5
+            from_core = jnp.where(m == 2, jnp.where(idx < 4, idx, 14), jnp.where(m == 0, 4 + idx, 9 + idx)) % 2
+            hand = remote(gw.at[k], gw.at[k], ssf.at[k], rsf.at[k], other)
+            if arriving:
+                @pl.when(ok & (from_core == core) & ((base + k != row) | jnp.logical_not(real)))
+                def _():
+                    remote(gb, gw.at[k], ssg.at[k], rsg.at[k], other).wait_recv()
+                @pl.when(ok & (from_core == core))
+                def _():
+                    hand.start()
+                @pl.when(jnp.logical_not(ok))
+                def _():
+                    gw[k] = jnp.zeros((NB, 128), BF16)
+            else:
+                @pl.when(ok & (from_core != core))
+                def _():
+                    hand.wait_recv()
+                @pl.when(ok & (from_core == core))
+                def _():
+                    hand.wait_send()
 
     def source(k):
         return matrix_of(member(k // 2, k % 2))
@@ -467,36 +509,22 @@
         copy_c(d).start()
     copy_d(0).start()
     extra[...] = tot[...]
+    window(True)
     for d in (1, 7, 2, 6, 3, 5, 4):
         copy_c(d).wait_recv()
         copy_d(d).start()
     for d in range(8):
         copy_d(d).wait_recv()
+    window(False)
     for k in range(8):
         for m in range(3):
             cols[m, 2 * k + core] = pc[0, k, m]
             cols[m, 2 * k + 1 - core] = pc[1, k, m]
 
-    a = p % 4
-    base = 15 * (p // 4) + jnp.where(a == 0, -1, jnp.where(a == 1, 3, jnp.where(a == 2, 7, 10)))
-    for k in range(6):
-        if k == 0:
-            ok = p > 0
-        elif k == 5:
-            ok = (a == 0) | ((a == 3) & (p < 63))
-        else:
-            ok = p >= 0
-        @pl.when(ok & ((base + k != row) | jnp.logical_not(real)))
-        def _():
-            remote(g, gw.at[k], ssg.at[k], rsg.at[k], other).wait_recv()
-        @pl.when(jnp.logical_not(ok))
-        def _():
-            gw[k] = jnp.zeros((NB, 128), F32)
-
     def wait_row(owner, k, ok, rr, n):
         @pl.when(ok & ((owner != p) | (rr != r)))
         def _():
-            remote(g, gw.at[k], ssg.at[n], rsg.at[k], {"rep": rr, "dp": owner}).wait_send()
+            remote(gb, gw.at[k], ssg.at[n], rsg.at[k], {"rep": rr, "dp": owner}).wait_send()
 
     give(wait_row)
     for d in range(1, 16):
@@ -551,7 +579,7 @@
         in_specs=[vm, vm, hbm, hbm, vm, vm],
         out_specs=[vm, vm, vm],
         out_shape=[
-            jax.ShapeDtypeStruct((6, NB, 128), F32),
+            jax.ShapeDtypeStruct((6, NB, 128), BF16),
             jax.ShapeDtypeStruct((3, 16, 8, 128), F32),
             jax.ShapeDtypeStruct((3, 8, 128), F32),
         ],
@@ -575,6 +603,7 @@
             pltpu.VMEM((n, 7, 16, 128), F32),
             pltpu.VMEM((128, RB), BF16),
             pltpu.VMEM((NB, 128), F32),
+            pltpu.VMEM((NB, 128), BF16),
             pltpu.VMEM((16, 8, 128), F32),
             pltpu.VMEM((15, 8, 128), F32),
             pltpu.VMEM((3, 8, 128), F32),
@@ -584,7 +613,7 @@
             dma(n), dma(n),
             dma(7), dma(3), dma(12), dma(12), dma(9), dma(9), dma(24), dma(24), dma(48), dma(48),
             dma(2 * n), dma(2 * n), dma(2 * n, 6), dma(2 * n, 6), dma(2 * n, 6), dma(2 * n, 6), dma(n, 7), dma(n, 7),
-            dma(15), dma(15), dma(15), dma(15), dma(7), dma(7), dma(8), dma(8), dma(24), dma(6),
+            dma(15), dma(15), dma(15), dma(15), dma(7), dma(7), dma(8), dma(8), dma(12), dma(6), dma(6), dma(6),
         ],
         compiler_params=pltpu.CompilerParams(
             vmem_limit_bytes=VMEM_LIMIT, collective_id=0, has_side_effects=True
@@ -593,7 +622,7 @@
     )(tokens.T, upstream.T, gate_pre, up_pre, quarter, wext)
 
 
-def update_kernel(lengths, gw, cols, extra, params, row_state, col_state, out_p, out_d, out_r, out_c, moved, scaled):
+def update_kernel(lengths, gw, cols, extra, params, row_state, col_state, out_p, out_d, out_r, out_c, moved, scaled, held):
     p = lax.axis_index("dp")
     start, length = span(lengths)
     a = p % 4
@@ -606,8 +635,11 @@
     lane = lax.broadcasted_iota(jnp.int32, (1, 128), 1)
     sums_row = extra[:, 7, :]
     live = lax.broadcasted_iota(jnp.int32, (3, 128), 1) < RB
-    rows = jnp.where(live, BETA * row_state[...] + (1.0 - BETA) * (sums_row * (1.0 / 14336.0) + TINY), 0.0)
-    out_r[...] = rows
+    for m in range(3):
+        held[m : m + 1, 0:RB] = row_state[:, m * RB : m * RB + RB]
+    rows = jnp.where(live, BETA * held[...] + (1.0 - BETA) * (sums_row * (1.0 / 14336.0) + TINY), 0.0)
+    for m in range(3):
+        out_r[:, m * RB : m * RB + RB] = rows[m : m + 1, 0:RB]
     means = jnp.sum(rows, axis=1, keepdims=True) * (1.0 / RB)
     weight = jnp.sum(sums_row, axis=0, keepdims=True)
     for k in range(6):
@@ -619,7 +651,7 @@
         sq = jnp.sum(jnp.where(lane == 120 + m, weight, 0.0), axis=1, keepdims=True)
         scale = RHO * jnp.sqrt(sq * (1.0 / (RB * 14336.0)))
         factor = value / pick(means)
-        v = gw[k] * lax.rsqrt(factor * out_c[pl.ds(pl.multiple_of(m * NB, 8), NB), :])
+        v = gw[k].astype(F32) * lax.rsqrt(factor * out_c[pl.ds(pl.multiple_of(m * NB, 8), NB), :])
         moved[pl.ds(k * NB, NB), :] = v
         scaled[pl.ds(k * NB, NB), :] = scale * v
     def tile(t, carry):
@@ -642,10 +674,10 @@
         out_shape=[
             jax.ShapeDtypeStruct((544, 128), BF16),
             jax.ShapeDtypeStruct((544, 128), BF16),
-            jax.ShapeDtypeStruct((3, 128), F32),
+            jax.ShapeDtypeStruct((1, 240), F32),
             jax.ShapeDtypeStruct((336, 128), F32),
         ],
-        scratch_shapes=[pltpu.VMEM((800, 128), F32), pltpu.VMEM((800, 128), F32)],
+        scratch_shapes=[pltpu.VMEM((800, 128), F32), pltpu.VMEM((800, 128), F32), pltpu.VMEM((3, 128), F32)],
         compiler_params=pltpu.CompilerParams(vmem_limit_bytes=VMEM_LIMIT),
         name="update",
     )(lengths, gw, cols, extra, params, row_state, col_state)
@@ -654,11 +686,10 @@
 def body(tokens, upstream, gate_pre, up_pre, param_shards, shard_rows, row_state, col_state):
     quarter, wext = prep(shard_rows, param_shards)
     gw, cols, extra = main(tokens, upstream, gate_pre, up_pre, quarter, wext)
-    row_in = jnp.pad(row_state.reshape(3, RB), ((0, 0), (0, 128 - RB)))
     new_params, direction, rows, new_cols = update(
-        shard_rows, gw, cols, extra, param_shards, row_in, col_state.reshape(336, 128)
+        shard_rows, gw, cols, extra, param_shards, row_state.reshape(1, 240), col_state.reshape(336, 128)
     )
-    return (new_params, direction, rows[:, :RB].reshape(-1), new_cols.reshape(-1))
+    return (new_params, direction, rows.reshape(-1), new_cols.reshape(-1))
 
 
 def solution(mesh):

time: 121 us -> 110 us (0.909)
  Pallas kernels: 117 us -> 109 us
  local copies, waits for them, and re-layouts: 2.67 us -> 0 us
    pallas_call x1, Pallas kernels: 113 us -> 104 us  [main(): pl.pallas_call(main_kernel, in_specs=[vm, vm, hbm, hbm, vm, vm], out_spec...]
    reshape x2 -> x0, local copies, waits for them, and re-layouts: 2.07 us -> none  [the longest x1 1.31 us: body(): rows[:, :RB].reshape(-1)]
where the time goes in v4:
time: 110 us
  Pallas kernels  109 us (99%)
    pallas_call x1, Pallas kernels, main(): pl.pallas_call(main_kernel, in_specs=[vm, vm, hbm, hbm, vm, vm], out_spec...  104 us
    pallas_call x1, Pallas kernels, update(): pl.pallas_call(update_kernel, in_specs=[pl.BlockSpec(memory_space=pltpu.S...  2.62 us

profile of v4, /device:TPU:1, one launch (start us, length us, event | category | flops | bytes accessed | tf_op | source)
XLA Modules:
  0.0 109.7 jit_solution(15235597485654990689)
XLA Ops:
  0.6 2.0 %prep.1 = (bf16[144,128]{1,0:T(8,128)(2,1)}, f32[8,128]{1,0:T(8,128)}) custom-call(s32[64]{0:T(128)} %lengths.3, bf16[544,128]{1,0:T(8,128)(2,1)} %params.3), custom_call_target="tpu_custom_call" | custom-call | tf_op jit(solution)/shard_map/prep/pallas_call | solution.py:81
  2.6 104.4 %main.1 = (bf16[6,112,128]{2,1,0:T(8,128)(2,1)}, f32[3,16,8,128]{3,2,1,0:T(8,128)}, f32[3,8,128]{2,1,0:T(8,128)}) custom-call(bf16[80,128]{1,0:T(8,128)(2,1)} %bitcast.7, bf16[80,128]{1,0:T(8,128)(2,1)} %bitcast.8, bf16[128,14336]{1,0:T(8,128)(2,1)} %gate_hbm.1, bf16[128,14336]{1,0:T(8,128)(2,1)} %upp_hbm.1, bf16[144,128]{1,0:T(8,128)(2,1)} %get-tuple-element.13.quarter, ...), custom_call_target="tpu_custom_call" | custom-call | tf_op jit(solution)/shard_map/main/pallas_call | solution.py:577
  107.0 2.6 %update.1 = (bf16[544,128]{1,0:T(8,128)(2,1)}, bf16[544,128]{1,0:T(8,128)(2,1)}, f32[1,240]{1,0:T(1,128)}, f32[336,128]{1,0:T(8,128)}) custom-call(s32[64]{0:T(128)} %lengths.3, bf16[6,112,128]{2,1,0:T(8,128)(2,1)} %get-tuple-element.15.gw, f32[3,16,8,128]{3,2,1,0:T(8,128)} %get-tuple-element.16.cols, f32[3,8,128]{2,1,0:T(8,128)} %get-tuple-element.17.extra, ...), custom_call_target="tpu_custom_call" | custom-call | tf_op jit(solution)/shard_map/update/pallas_call | solution.py:670

commit v5 on v4

--- a/solution.py
+++ b/solution.py
@@ -177,22 +177,34 @@
                 remote(quarter, w.at[z, r, u], w1.at[0], v1.at[u], spread(1)).wait_recv()
             copy_up(1, u).start()
             copy_down(1, u).start()
+        for u in range(3):
             copy_y(0, u).start()
+        for u in range(3):
             copy_core(0, r, u).start()
 
     def gather_ring(s):
         for u in range(3):
-            copy_up(s, u).wait_recv()
+            for copy, last in ((copy_up, u < 2), (copy_down, u == 2)):
+                if s < 4 or last:
+                    copy(s, u).wait_recv()
+                if s < 3 or (s == 3 and last):
+                    copy(s + 1, u).start()
+        for u in range(3):
+            copy_y(s, u).start()
             if s < 4:
-                copy_up(s + 1, u).start()
-            copy_y(s, u).start()
+                copy_y(8 - s, u).start()
+        for u in range(3):
             copy_core(s, r, u).start()
             if s < 4:
-                copy_down(s, u).wait_recv()
-                if s < 3:
-                    copy_down(s + 1, u).start()
-                copy_y(8 - s, u).start()
                 copy_core(8 - s, r, u).start()
+        hand_over(s - 1)
+        if s > 1:
+            hand_over(9 - s)
+
+    def hand_over(k):
+        for u in range(3):
+            copy_y(k, u).wait_recv()
+            copy_core(k, mate, u).start()
 
     f, c1, a1, c2 = (fa, fb), (c1a, c1b), (a1a, a1b), (c2a, c2b)
     a2, own2, c3 = (a2a, a2b), (own2a, own2b), (c3a, c3b)
@@ -287,7 +299,12 @@
             for b in range(2):
                 rows[pl.ds(jj * 2 + b, RB, stride=16), :] = gd[:, b * 128 : b * 128 + 128]
             return carry
-        lax.fori_loop(0, 8, block, 0, unroll=4)
+        for half in range(2):
+            lax.fori_loop(0, 4, lambda jj, k: block(jj + 4 * half, k), 0, unroll=4)
+            if half == 0:
+                @pl.when(c > 0)
+                def _():
+                    step1(0, c - 1)
         def pack(big, carry):
             for idx in range(5):
                 at = pl.ds(pl.multiple_of((big * 5 + idx) * 16, 16), 16)
@@ -295,9 +312,6 @@
             return carry
         lax.fori_loop(0, 16, pack, 0, unroll=2)
         copy1(0, c).start()
-        @pl.when(c > 0)
-        def _():
-            step1(0, c - 1)
         for at, what in ((2, gather_first), (3, lambda: gather_ring(1)), (5, lambda: gather_ring(2))):
             @pl.when(c == at)
             def _():
@@ -306,19 +320,8 @@
 
     lax.fori_loop(0, PIECES, phase_a, 0)
     step1(0, PIECES - 1)
-    gather_ring(3)
-    for c in range(4):
-        step2(0, c)
-    gather_ring(4)
-    for c in range(4, PIECES):
-        step2(0, c)
-
-    def build(j, carry):
-        k = jnp.where(j % 2 == 1, (j + 1) // 2, (8 - j // 2) % 8)
+    def build(k):
         o = (z + 8 - k) % 8
-        for u in range(3):
-            copy_y(k, u).wait_recv()
-            copy_core(k, mate, u).start()
         for u in range(3):
             copy_core(k, r, u).wait_recv()
             copy_core(k, mate, u).wait_recv()
@@ -333,9 +336,19 @@
                             wflat[pl.ds(off + at, 8), :] = v[half * 8 : half * 8 + 8]
                         else:
                             wflat[pl.ds(off + at, 8), :] += v[half * 8 : half * 8 + 8]
-        return carry
-
-    lax.fori_loop(0, 8, build, 0)
+    gather_ring(3)
+    build(0)
+    for c in range(4):
+        step2(0, c)
+    gather_ring(4)
+    for k in (1, 7):
+        build(k)
+    for c in range(4, PIECES):
+        step2(0, c)
+    hand_over(4)
+    for k in (2, 6, 3, 5, 4):
+        build(k)
+
 
     def phase_b(c, carry):
         def block(jj, carry):
@@ -351,7 +364,12 @@
                 for b in range(2):
                     rows[pl.ds(m * RB * 16 + jj * 2 + b, RB, stride=16), :] = v[:, b * 128 : b * 128 + 128]
             return carry
-        lax.fori_loop(0, 8, block, 0, unroll=4)
+        for half in range(2):
+            lax.fori_loop(0, 4, lambda jj, k: block(jj + 4 * half, k), 0, unroll=4)
+            if half == 0:
+                @pl.when(c > 0)
+                def _():
+                    step1(1, c - 1)
         def pack(big, carry):
             for n in range(4, 14):
                 row = (n - 4) // 5 * RB + (n - 4) % 5
@@ -361,9 +379,6 @@
         lax.fori_loop(0, 16, pack, 0, unroll=2)
         copy1(1, c).start()
         step3(0, c)
-        @pl.when(c > 0)
-        def _():
-            step1(1, c - 1)
         @pl.when(c > 2)
         def _():
             step2(1, c - 3)
@@ -509,10 +524,10 @@
         copy_c(d).start()
     copy_d(0).start()
     extra[...] = tot[...]
-    window(True)
     for d in (1, 7, 2, 6, 3, 5, 4):
         copy_c(d).wait_recv()
         copy_d(d).start()
+    window(True)
     for d in range(8):
         copy_d(d).wait_recv()
     window(False)
@@ -542,8 +557,9 @@
 
     for u in range(3):
         for s in range(1, 5):
-            copy_up(s, u).wait_send()
-            if s < 4:
+            if s < 4 or u < 2:
+                copy_up(s, u).wait_send()
+            if s < 4 or u == 2:
                 copy_down(s, u).wait_send()
 
     def drain_w(k, carry):
@@ -611,7 +627,7 @@
             pltpu.VMEM((3, 8, 128), F32),
             pltpu.VMEM((2, 8, 3, 8, 128), F32),
             dma(n), dma(n),
-            dma(7), dma(3), dma(12), dma(12), dma(9), dma(9), dma(24), dma(24), dma(48), dma(48),
+            dma(7), dma(3), dma(12), dma(12), dma(12), dma(12), dma(24), dma(24), dma(48), dma(48),
             dma(2 * n), dma(2 * n), dma(2 * n, 6), dma(2 * n, 6), dma(2 * n, 6), dma(2 * n, 6), dma(n, 7), dma(n, 7),
             dma(15), dma(15), dma(15), dma(15), dma(7), dma(7), dma(8), dma(8), dma(12), dma(6), dma(6), dma(6),
         ],

time: 110 us -> 106 us (0.964)
  Pallas kernels: 109 us -> 105 us
    pallas_call x1, Pallas kernels: 104 us -> 101 us  [main(): pl.pallas_call(main_kernel, in_specs=[vm, vm, hbm, hbm, vm, vm], out_spec...]
where the time goes in v5:
time: 106 us
  Pallas kernels  105 us (99%)
    pallas_call x1, Pallas kernels, main(): pl.pallas_call(main_kernel, in_specs=[vm, vm, hbm, hbm, vm, vm], out_spec...  101 us
    pallas_call x1, Pallas kernels, update(): pl.pallas_call(update_kernel, in_specs=[pl.BlockSpec(memory_space=pltpu.S...  2.62 us

profile of v5, /device:TPU:1, one launch (start us, length us, event | category | flops | bytes accessed | tf_op | source)
XLA Modules:
  0.0 105.8 jit_solution(2714142457175293458)
XLA Ops:
  0.6 2.0 %prep.1 = (bf16[144,128]{1,0:T(8,128)(2,1)}, f32[8,128]{1,0:T(8,128)}) custom-call(s32[64]{0:T(128)} %lengths.3, bf16[544,128]{1,0:T(8,128)(2,1)} %params.3), custom_call_target="tpu_custom_call" | custom-call | tf_op jit(solution)/shard_map/prep/pallas_call | solution.py:81
  2.6 100.6 %main.1 = (bf16[6,112,128]{2,1,0:T(8,128)(2,1)}, f32[3,16,8,128]{3,2,1,0:T(8,128)}, f32[3,8,128]{2,1,0:T(8,128)}) custom-call(bf16[80,128]{1,0:T(8,128)(2,1)} %bitcast.7, bf16[80,128]{1,0:T(8,128)(2,1)} %bitcast.8, bf16[128,14336]{1,0:T(8,128)(2,1)} %gate_hbm.1, bf16[128,14336]{1,0:T(8,128)(2,1)} %upp_hbm.1, bf16[144,128]{1,0:T(8,128)(2,1)} %get-tuple-element.13.quarter, ...), custom_call_target="tpu_custom_call" | custom-call | tf_op jit(solution)/shard_map/main/pallas_call | solution.py:593
  103.2 2.6 %update.1 = (bf16[544,128]{1,0:T(8,128)(2,1)}, bf16[544,128]{1,0:T(8,128)(2,1)}, f32[1,240]{1,0:T(1,128)}, f32[336,128]{1,0:T(8,128)}) custom-call(s32[64]{0:T(128)} %lengths.3, bf16[6,112,128]{2,1,0:T(8,128)(2,1)} %get-tuple-element.15.gw, f32[3,16,8,128]{3,2,1,0:T(8,128)} %get-tuple-element.16.cols, f32[3,8,128]{2,1,0:T(8,128)} %get-tuple-element.17.extra, ...), custom_call_target="tpu_custom_call" | custom-call | tf_op jit(solution)/shard_map/update/pallas_call | solution.py:686

commit v6 on v5

--- a/solution.py
+++ b/solution.py
@@ -468,6 +468,39 @@
     gb[...] = g[...].astype(BF16)
     give(send_row)
 
+    @pl.when(p >= 40)
+    def _():
+        for d in range(1, 8):
+            copy_spread(d).wait_send()
+
+    for u in range(3):
+        for s in range(1, 5):
+            if s < 4 or u < 2:
+                copy_up(s, u).wait_send()
+            if s < 4 or u == 2:
+                copy_down(s, u).wait_send()
+
+    def drain_w(k, carry):
+        for u in range(3):
+            copy_y(k, u).wait_send()
+            copy_core(k, r, u).wait_send()
+            copy_core(k, mate, u).wait_send()
+        return carry
+
+    def drain(c, carry):
+        for t in range(2):
+            copy1(t, c).wait_send()
+            for h in range(2):
+                for d in (1, 2, 3):
+                    copy2(t, c, h, d).wait_send()
+                    copy3(t, c, h, d).wait_send()
+        for d in range(1, 8):
+            copy4(c, d).wait_send()
+        return carry
+
+    lax.fori_loop(0, 8, drain_w, 0)
+    lax.fori_loop(0, PIECES, drain, 0)
+
     a = p % 4
     base = 15 * (p // 4) + jnp.where(a == 0, -1, jnp.where(a == 1, 3, jnp.where(a == 2, 7, 10)))
 
@@ -515,6 +548,8 @@
             acc[m] += jnp.where(m_src == m, v, 0.0)
     for d in range(1, 16):
         copy_b(d).start()
+    for d in range(1, 16):
+        copy_a(d).wait_send()
     tot[...] = acc[...]
     for d in range(1, 16):
         copy_b(d).wait_recv()
@@ -524,6 +559,15 @@
         copy_c(d).start()
     copy_d(0).start()
     extra[...] = tot[...]
+
+    def wait_row(owner, k, ok, rr, n):
+        @pl.when(ok & ((owner != p) | (rr != r)))
+        def _():
+            remote(gb, gw.at[k], ssg.at[n], rsg.at[k], {"rep": rr, "dp": owner}).wait_send()
+
+    give(wait_row)
+    for d in range(1, 16):
+        copy_b(d).wait_send()
     for d in (1, 7, 2, 6, 3, 5, 4):
         copy_c(d).wait_recv()
         copy_d(d).start()
@@ -535,53 +579,10 @@
         for m in range(3):
             cols[m, 2 * k + core] = pc[0, k, m]
             cols[m, 2 * k + 1 - core] = pc[1, k, m]
-
-    def wait_row(owner, k, ok, rr, n):
-        @pl.when(ok & ((owner != p) | (rr != r)))
-        def _():
-            remote(gb, gw.at[k], ssg.at[n], rsg.at[k], {"rep": rr, "dp": owner}).wait_send()
-
-    give(wait_row)
-    for d in range(1, 16):
-        copy_a(d).wait_send()
-        copy_b(d).wait_send()
     for d in range(8):
         if d:
             copy_c(d).wait_send()
         copy_d(d).wait_send()
-
-    @pl.when(p >= 40)
-    def _():
-        for d in range(1, 8):
-            copy_spread(d).wait_send()
-
-    for u in range(3):
-        for s in range(1, 5):
-            if s < 4 or u < 2:
-                copy_up(s, u).wait_send()
-            if s < 4 or u == 2:
-                copy_down(s, u).wait_send()
-
-    def drain_w(k, carry):
-        for u in range(3):
-            copy_y(k, u).wait_send()
-            copy_core(k, r, u).wait_send()
-            copy_core(k, mate, u).wait_send()
-        return carry
-
-    def drain(c, carry):
-        for t in range(2):
-            copy1(t, c).wait_send()
-            for h in range(2):
-                for d in (1, 2, 3):
-                    copy2(t, c, h, d).wait_send()
-                    copy3(t, c, h, d).wait_send()
-        for d in range(1, 8):
-            copy4(c, d).wait_send()
-        return carry
-
-    lax.fori_loop(0, 8, drain_w, 0)
-    lax.fori_loop(0, PIECES, drain, 0)
 
 
 def main(tokens, upstream, gate_pre, up_pre, quarter, wext):

time: 106 us -> 105 us (level)
  no operation moved by 1% of the time
where the time goes in v6:
time: 105 us
  Pallas kernels  105 us (100%)
    pallas_call x1, Pallas kernels, main(): pl.pallas_call(main_kernel, in_specs=[vm, vm, hbm, hbm, vm, vm], out_spec...  99.9 us
    pallas_call x1, Pallas kernels, update(): pl.pallas_call(update_kernel, in_specs=[pl.BlockSpec(memory_space=pltpu.S...  2.62 us

profile of v6, /device:TPU:1, one launch (start us, length us, event | category | flops | bytes accessed | tf_op | source)
XLA Modules:
  0.0 105.2 jit_solution(17576277433000547139)
XLA Ops:
  0.6 2.0 %prep.1 = (bf16[144,128]{1,0:T(8,128)(2,1)}, f32[8,128]{1,0:T(8,128)}) custom-call(s32[64]{0:T(128)} %lengths.3, bf16[544,128]{1,0:T(8,128)(2,1)} %params.3), custom_call_target="tpu_custom_call" | custom-call | tf_op jit(solution)/shard_map/prep/pallas_call | solution.py:81
  2.6 99.9 %main.1 = (bf16[6,112,128]{2,1,0:T(8,128)(2,1)}, f32[3,16,8,128]{3,2,1,0:T(8,128)}, f32[3,8,128]{2,1,0:T(8,128)}) custom-call(bf16[80,128]{1,0:T(8,128)(2,1)} %bitcast.7, bf16[80,128]{1,0:T(8,128)(2,1)} %bitcast.8, bf16[128,14336]{1,0:T(8,128)(2,1)} %gate_hbm.1, bf16[128,14336]{1,0:T(8,128)(2,1)} %upp_hbm.1, bf16[144,128]{1,0:T(8,128)(2,1)} %get-tuple-element.13.quarter, ...), custom_call_target="tpu_custom_call" | custom-call | tf_op jit(solution)/shard_map/main/pallas_call | solution.py:594
  102.5 2.6 %update.1 = (bf16[544,128]{1,0:T(8,128)(2,1)}, bf16[544,128]{1,0:T(8,128)(2,1)}, f32[1,240]{1,0:T(1,128)}, f32[336,128]{1,0:T(8,128)}) custom-call(s32[64]{0:T(128)} %lengths.3, bf16[6,112,128]{2,1,0:T(8,128)(2,1)} %get-tuple-element.15.gw, f32[3,16,8,128]{3,2,1,0:T(8,128)} %get-tuple-element.16.cols, f32[3,8,128]{2,1,0:T(8,128)} %get-tuple-element.17.extra, ...), custom_call_target="tpu_custom_call" | custom-call | tf_op jit(solution)/shard_map/update/pallas_call | solution.py:687
